TPU v7x, 512 devices: a whole 4x8x8 slice. The times are simulated.
512 devices in a mesh: dp: 64 (over x, y, core), shard: 8 (over z).
Axes of the slice: x: 4, y: 8, z: 8, core: 2. Of those that a mesh axis runs over, the one named last changes fastest.
Arguments:
- grads: bfloat16 [8, 4096, 512], P('shard', 'dp')
- left_old: float32 [8, 4096, 512], P('shard', 'dp'), as said below
- right_old: float32 [8, 4096, 512], P('shard', 'dp'), as said below
- root_steps: int32 [8, 8, 2], P('shard'), may hold values from 1 to 3, as said below
Outputs:
- update: bfloat16 [8, 4096, 512], P('shard')
- left_new: float32 [8, 4096, 512], P('shard', 'dp')
- right_new: float32 [8, 4096, 512], P('shard', 'dp')
Inputs may be any that keep to these rules, and one draw needn't show every extreme that they name: `root_steps`: every entry is 1, 2 or 3; in every draw some entry is 1 and some entry is 3. `left_old`: every block is symmetric and positive definite. `right_old`: every block is symmetric and positive definite.
All inputs are finite; a program needn't handle non-finite values.
Results may differ from a plain program's by a relative error of at most 0.0045.
Values may be sent and summed in bfloat16 or wider, within the bound.
No kernel may reach another device: no remote copies, remote signals or barrier semaphores. Data moves between devices by JAX's collectives and lax.ppermute only.
A program may use at most 64 MiB of HBM per device.

v0:
```python
import jax
import jax.numpy as jnp
from jax import lax
from jax.sharding import PartitionSpec as P

GROUP = 8


epsilon = 1e-06
decay_rate = 0.95


def partner(shard, axis, stride):
    return lax.ppermute(shard, axis, [(i, i ^ 1 << stride) for i in range(lax.axis_size(axis))])


def shortened(shard):
    return jax.tree.map(lambda a: a.astype(jnp.bfloat16) if a.dtype == jnp.float32 else a, shard)


def precise_dot(left, right):
    return jnp.dot(left, right, precision=lax.Precision.HIGHEST, preferred_element_type=jnp.float32)


def stitch(mine, partner_part, upper_half, axis_index):
    lower_rows = jnp.where(upper_half, partner_part, mine)
    upper_rows = jnp.where(upper_half, mine, partner_part)
    return jnp.concatenate([lower_rows, upper_rows], axis=axis_index)


def group_gather(portion, bit_list, position, swapper, axis_index):
    for bit_index in bit_list:
        partner_part = swapper(portion, bit_index)
        upper_half = position >> bit_index & 1 == 1
        portion = jax.tree.map(
            lambda mine, other_side: stitch(mine, other_side, upper_half, axis_index),
            portion,
            partner_part,
        )
    return portion


def per_device(grads, left_old, right_old, root_steps):
    position = lax.axis_index("dp")
    member = position % GROUP
    block_in_stack = position // GROUP
    is_right = member >= GROUP // 2
    slab_rows = grads.shape[1]
    extent = grads.shape[2]
    grad_rows = grads[0]
    full_grad = group_gather(
        grad_rows, (0, 1, 2), position, lambda value, bit_index: partner(value, "dp", bit_index), 0
    )
    first_row = member * slab_rows
    columns = lax.dynamic_slice_in_dim(full_grad, first_row, slab_rows, 1)
    left_rows = decay_rate * left_old[0] + lax.dot_general(
        grad_rows, full_grad, (((1,), (1,)), ((), ())), preferred_element_type=jnp.float32
    )
    right_rows = decay_rate * right_old[0] + lax.dot_general(
        columns, full_grad, (((0,), (0,)), ((), ())), preferred_element_type=jnp.float32
    )
    full_left, full_right = group_gather(
        (left_rows, right_rows),
        (0, 1, 2),
        position,
        lambda value, bit_index: jax.tree.map(
            lambda part, own: part.astype(own.dtype),
            partner(shortened(value), "dp", bit_index),
            value,
        ),
        0,
    )
    factor = jnp.where(is_right, full_right, full_left)
    pair_counts = lax.dynamic_index_in_dim(root_steps[0], block_in_stack, 0, keepdims=False)
    step_count = jnp.where(is_right, pair_counts[1], pair_counts[0])
    identity = jnp.eye(extent, dtype=jnp.float32)
    magnitude = jnp.sqrt(jnp.sum(factor * factor) + epsilon)
    scaling = 2.5 / magnitude

    def newton(iteration, carry_pair):
        matrix, inverse = carry_pair
        shifted = (5.0 * identity - matrix) * 0.25
        inverse = precise_dot(inverse, shifted)
        square = precise_dot(shifted, shifted)
        fourth = precise_dot(square, square)
        return (precise_dot(fourth, matrix), inverse)

    carry_pair = lax.fori_loop(
        0, step_count, newton, (scaling * factor, jnp.sqrt(jnp.sqrt(scaling)) * identity)
    )
    own_root = carry_pair[1]
    partner_root = partner(own_root, "dp", 2)
    left_root = jnp.where(is_right, partner_root, own_root)
    right_root = jnp.where(is_right, own_root, partner_root)
    left_slab = lax.dynamic_slice_in_dim(left_root, first_row, slab_rows, 0)
    conditioned = precise_dot(precise_dot(left_slab, full_grad.astype(jnp.float32)), right_root)
    totals = lax.psum(
        (jnp.sum(jnp.square(grad_rows.astype(jnp.float32))), jnp.sum(conditioned * conditioned)),
        ("dp", "shard"),
    )
    graft_ratio = jnp.sqrt(totals[0] / (totals[1] + epsilon))
    scaled = (conditioned * graft_ratio).astype(jnp.bfloat16)
    update = lax.all_gather(scaled[None], "dp", axis=1, tiled=True)
    return (update, left_rows[None], right_rows[None])


def solution(mesh):
    placed = (
        P("shard", "dp", None),
        P("shard", "dp", None),
        P("shard", "dp", None),
        P("shard", None, None),
    )
    return jax.shard_map(
        per_device,
        mesh=mesh,
        in_specs=placed,
        out_specs=(P("shard", None, None), P("shard", "dp", None), P("shard", "dp", None)),
        check_vma=False,
    )
```

profile of v0, /device:TPU:1, one launch (start us, length us, event | category | flops | bytes accessed | tf_op | source)
XLA Modules:
  0.0 352.3 jit_solution(14758970879236495291)
XLA Ops:
  7.2 8.8 %collective-permute-start = (bf16[64,512]{1,0:T(8,128)(2,1)}, bf16[64,512]{1,0:T(8,128)(2,1)S(1)}, u32[]{:S(2)}, u32[]{:S(2)}) collective-permute-start(bf16[64,512]{1,0:T(8,128)(2,1)} %bitcast.43), channel_id=1, source_target_pairs={{0,8},{8,0},{16,24},{24,16},{32,40},{40,32},{48,56},{56,48},{64,72... | collective-permute-start | bytes 196616 | tf_op jit(solution)/shard_map/ppermute | solution.py:14
  16.0 1.1 collective-permute-done
  17.1 0.9 broadcast_select_fusion.5
  18.0 1.9 collective-permute-start.1
  19.9 4.7 %collective-permute-done.1 = bf16[128,512]{1,0:T(8,128)(2,1)S(1)} collective-permute-done((bf16[128,512]{1,0:T(8,128)(2,1)S(1)}, bf16[128,512]{1,0:T(8,128)(2,1)S(1)}, u32[]{:S(2)}, u32[]{:S(2)}) %collective-permute-start.1) | collective-permute-done | bytes 131104 | tf_op jit(solution)/shard_map/ppermute | solution.py:14
  24.7 1.9 collective-permute-start.2
  26.6 14.6 %collective-permute-done.2 = bf16[256,512]{1,0:T(8,128)(2,1)S(1)} collective-permute-done((bf16[256,512]{1,0:T(8,128)(2,1)S(1)}, bf16[256,512]{1,0:T(8,128)(2,1)S(1)}, u32[]{:S(2)}, u32[]{:S(2)}) %collective-permute-start.2) | collective-permute-done | bytes 262176 | tf_op jit(solution)/shard_map/ppermute | solution.py:14
  41.3 0.1 broadcast_select_fusion.1
  41.4 1.3 fusion.39
  42.7 2.5 collective-permute-start.6
  45.2 1.2 fusion.40
  46.4 1.9 collective-permute-start.3
  48.4 1.2 collective-permute-done.3
  49.6 0.1 convert_select_fusion.9
  49.7 1.9 collective-permute-start.4
  51.6 0.1 constant_dynamic-slice_fusion
  51.7 3.4 collective-permute-start.7
  55.1 1.4 collective-permute-done.4
  56.5 0.1 convert_select_fusion.7
  56.6 1.9 collective-permute-start.5
  58.5 0.8 collective-permute-done.7
  59.3 0.1 convert_select_fusion.5
  59.4 3.5 collective-permute-start.8
  62.9 0.6 fusion.38
  64.8 14.1 %collective-permute-done.5 = bf16[256,512]{1,0:T(8,128)(2,1)S(1)} collective-permute-done((bf16[256,512]{1,0:T(8,128)(2,1)S(1)}, bf16[256,512]{1,0:T(8,128)(2,1)S(1)}, u32[]{:S(2)}, u32[]{:S(2)}) %collective-permute-start.5) | collective-permute-done | bytes 262176 | tf_op jit(solution)/shard_map/ppermute | solution.py:14
  78.8 0.1 convert_select_fusion.3
  79.0 5.6 %collective-permute-done.8 = bf16[256,512]{1,0:T(8,128)(2,1)} collective-permute-done((bf16[256,512]{1,0:T(8,128)(2,1)S(1)}, bf16[256,512]{1,0:T(8,128)(2,1)}, u32[]{:S(2)}, u32[]{:S(2)}) %collective-permute-start.8) | collective-permute-done | bytes 262176 | tf_op jit(solution)/shard_map/ppermute | solution.py:14
  84.5 1.1 convert_select_fusion.1
  85.6 0.9 multiply_reduce_fusion
  87.3 0.2 broadcast_multiply_fusion
  87.6 0.1 fusion.21
  87.7 7.7 %while.13 = (s32[]{:T(128)}, f32[512,512]{1,0:T(8,128)S(1)}, f32[512,512]{0,1:T(8,128)S(1)}, s32[]{:T(128)}, s32[]{:T(128)}) while((s32[]{:T(128)}, f32[512,512]{1,0:T(8,128)S(1)}, f32[512,512]{0,1:T(8,128)S(1)}, s32[]{:T(128)}, s32[]{:T(128)}) %tuple.40), condition=%wide.region_2.3_spmd.clone, body=%wide.region_1.2_spmd.clone.sunk | while | flops 6444548096 | bytes 14680125 | solution.py:88
  87.7 0.1 copy.24
  87.8 0.1 copy.25
  87.9 1.9 fusion.66
  89.8 1.8 fusion.67
  91.7 1.9 convolution_bitcast_fusion.3
  93.6 1.9 fusion.68
  95.4 0.3 copy.7
  95.8 16.5 %collective-permute-start.9 = (f32[512,512]{1,0:T(8,128)S(1)}, f32[512,512]{1,0:T(8,128)S(1)}, u32[]{:S(2)}, u32[]{:S(2)}) collective-permute-start(f32[512,512]{1,0:T(8,128)S(1)} %copy.7), channel_id=1, source_target_pairs={{0,32},{8,40},{16,48},{24,56},{32,0},{40,8},{48,16},{56,24},{64,96... | collective-permute-start | bytes 3145736 | tf_op jit(solution)/shard_map/ppermute | solution.py:14
  112.3 0.6 multiply_reduce_fusion.2
  113.0 45.4 %collective-permute-done.9 = f32[512,512]{1,0:T(8,128)S(1)} collective-permute-done((f32[512,512]{1,0:T(8,128)S(1)}, f32[512,512]{1,0:T(8,128)S(1)}, u32[]{:S(2)}, u32[]{:S(2)}) %collective-permute-start.9) | collective-permute-done | bytes 1048608 | tf_op jit(solution)/shard_map/ppermute | solution.py:14
  158.4 0.4 fusion.27
  158.7 1.4 multiply_reduce_fusion.1
  160.1 99.3 %all-reduce = (f32[]{:T(128)}, f32[]{:T(128)}) all-reduce(f32[]{:T(128)} %multiply_reduce_fusion.2, f32[]{:T(128)} %get-tuple-element.77), channel_id=1, replica_groups=mesh['dp'=64,'shard'=8] {'dp','shard'}, use_global_device_ids=true, to_apply=%region_4.5 | all-reduce | flops 2 | bytes 16 | tf_op jit(solution)/shard_map/psum | solution.py:97
  260.8 0.6 multiply_convert_fusion
  261.4 79.6 %all-gather.3.cloned.1.call-done = bf16[4096,512]{1,0:T(8,128)(2,1)} async-done(((bf16[64,512]{1,0:T(8,128)(2,1)}), bf16[4096,512]{1,0:T(8,128)(2,1)}) %all-gather.3.cloned.1.call-update) | async-done | bytes 4194320 | tf_op jit(solution)/shard_map/all_gather | solution.py:103
  341.0 4.5 %copy.26 = bf16[1,4096,512]{2,1,0:T(8,128)(2,1)} copy(bf16[1,4096,512]{2,1,0:T(8,128)(2,1)} %bitcast.41) | data formatting | bytes 8388608
  (22 shorter events, 0.3 us)
Async XLA Ops:
  7.2 44.4 %copy-start = (s32[1,8,2]{1,2,0:T(2,128)S(1)}, s32[1,8,2]{1,2,0:T(2,128)}, u32[]{:S(2)}) copy-start(s32[1,8,2]{1,2,0:T(2,128)} %param.9) | copy-start | bytes 196
  7.2 333.8 %all-gather.3.cloned.1.call-start = ((), (), s32[]{:S(2)}) async-start(), calls=%async_computation | async-start | bytes 4259840 | tf_op jit(solution)/shard_map/all_gather | solution.py:103
  7.2 9.9 %collective-permute-start = (bf16[64,512]{1,0:T(8,128)(2,1)}, bf16[64,512]{1,0:T(8,128)(2,1)S(1)}, u32[]{:S(2)}, u32[]{:S(2)}) collective-permute-start(bf16[64,512]{1,0:T(8,128)(2,1)} %bitcast.43), channel_id=1, source_target_pairs={{0,8},{8,0},{16,24},{24,16},{32,40},{40,32},{48,56},{56,48},{64,72... | collective-permute-start | bytes 196616 | tf_op jit(solution)/shard_map/ppermute | solution.py:14
  18.0 6.6 %collective-permute-start.1 = (bf16[128,512]{1,0:T(8,128)(2,1)S(1)}, bf16[128,512]{1,0:T(8,128)(2,1)S(1)}, u32[]{:S(2)}, u32[]{:S(2)}) collective-permute-start(bf16[128,512]{1,0:T(8,128)(2,1)S(1)} %pad_maximum_fusion.9), channel_id=1, source_target_pairs={{0,16},{8,24},{16,0},{24,8},{32,48},{40,56},{48,32},{56,40},{64,80... | collective-permute-start | bytes 393224 | tf_op jit(solution)/shard_map/ppermute | solution.py:14
  24.7 16.6 %collective-permute-start.2 = (bf16[256,512]{1,0:T(8,128)(2,1)S(1)}, bf16[256,512]{1,0:T(8,128)(2,1)S(1)}, u32[]{:S(2)}, u32[]{:S(2)}) collective-permute-start(bf16[256,512]{1,0:T(8,128)(2,1)S(1)} %pad_maximum_fusion.3), channel_id=1, source_target_pairs={{0,32},{8,40},{16,48},{24,56},{32,0},{40,8},{48,16},{56,24},{64,96... | collective-permute-start | bytes 786440 | tf_op jit(solution)/shard_map/ppermute | solution.py:14
  41.4 3.8 %copy-start.1 = (bf16[256,512]{1,0:T(8,128)(2,1)}, bf16[256,512]{1,0:T(8,128)(2,1)S(1)}, u32[]{:S(2)}) copy-start(bf16[256,512]{1,0:T(8,128)(2,1)S(1)} %get-tuple-element.58) | copy-start | bytes 786436
  42.7 15.8 %copy-start.5 = (f32[64,512]{1,0:T(8,128)}, f32[64,512]{1,0:T(8,128)S(1)}, u32[]{:S(2)}) copy-start(f32[64,512]{1,0:T(8,128)S(1)} %get-tuple-element.74) | copy-start | bytes 393220
  42.7 5.7 %collective-permute-start.6 = (bf16[64,512]{1,0:T(8,128)(2,1)S(1)}, bf16[64,512]{1,0:T(8,128)(2,1)S(1)}, u32[]{:S(2)}, u32[]{:S(2)}) collective-permute-start(bf16[64,512]{1,0:T(8,128)(2,1)S(1)} %get-tuple-element.73), channel_id=1, source_target_pairs={{0,8},{8,0},{16,24},{24,16},{32,40},{40,32},{48,56},{56,48},{64,72... | collective-permute-start | bytes 196616 | tf_op jit(solution)/shard_map/ppermute | solution.py:14
  46.4 39.2 %copy-start.3 = (f32[64,512]{1,0:T(8,128)}, f32[64,512]{1,0:T(8,128)S(1)}, u32[]{:S(2)}) copy-start(f32[64,512]{1,0:T(8,128)S(1)} %get-tuple-element.76) | copy-start | bytes 393220
  46.4 3.1 collective-permute-start.3
  49.7 6.8 %collective-permute-start.4 = (bf16[128,512]{1,0:T(8,128)(2,1)S(1)}, bf16[128,512]{1,0:T(8,128)(2,1)S(1)}, u32[]{:S(2)}, u32[]{:S(2)}) collective-permute-start(bf16[128,512]{1,0:T(8,128)(2,1)S(1)} %fusion.26), channel_id=1, source_target_pairs={{0,16},{8,24},{16,0},{24,8},{32,48},{40,56},{48,32},{56,40},{64,80... | collective-permute-start | bytes 393224 | tf_op jit(solution)/shard_map/ppermute | solution.py:14
  51.7 7.6 %collective-permute-start.7 = (bf16[128,512]{1,0:T(8,128)(2,1)S(1)}, bf16[128,512]{1,0:T(8,128)(2,1)S(1)}, u32[]{:S(2)}, u32[]{:S(2)}) collective-permute-start(bf16[128,512]{1,0:T(8,128)(2,1)S(1)} %fusion.25), channel_id=1, source_target_pairs={{0,16},{8,24},{16,0},{24,8},{32,48},{40,56},{48,32},{56,40},{64,80... | collective-permute-start | bytes 393224 | tf_op jit(solution)/shard_map/ppermute | solution.py:14
  56.6 22.2 %collective-permute-start.5 = (bf16[256,512]{1,0:T(8,128)(2,1)S(1)}, bf16[256,512]{1,0:T(8,128)(2,1)S(1)}, u32[]{:S(2)}, u32[]{:S(2)}) collective-permute-start(bf16[256,512]{1,0:T(8,128)(2,1)S(1)} %fusion.24), channel_id=1, source_target_pairs={{0,32},{8,40},{16,48},{24,56},{32,0},{40,8},{48,16},{56,24},{64,96... | collective-permute-start | bytes 786440 | tf_op jit(solution)/shard_map/ppermute | solution.py:14
  59.4 25.1 %collective-permute-start.8 = (bf16[256,512]{1,0:T(8,128)(2,1)S(1)}, bf16[256,512]{1,0:T(8,128)(2,1)}, u32[]{:S(2)}, u32[]{:S(2)}) collective-permute-start(bf16[256,512]{1,0:T(8,128)(2,1)S(1)} %fusion.23), channel_id=1, source_target_pairs={{0,32},{8,40},{16,48},{24,56},{32,0},{40,8},{48,16},{56,24},{64,96... | collective-permute-start | bytes 786440 | tf_op jit(solution)/shard_map/ppermute | solution.py:14
  87.7 24.6 %copy-start.4 = (bf16[1,64,512]{2,1,0:T(8,128)(2,1)S(1)}, bf16[1,64,512]{2,1,0:T(8,128)(2,1)}, u32[]{:S(2)}) copy-start(bf16[1,64,512]{2,1,0:T(8,128)(2,1)} %param.6) | copy-start | bytes 196612
  87.7 70.7 %copy-start.2 = (bf16[256,512]{1,0:T(8,128)(2,1)S(1)}, bf16[256,512]{1,0:T(8,128)(2,1)}, u32[]{:S(2)}) copy-start(bf16[256,512]{1,0:T(8,128)(2,1)} %copy-done.1) | copy-start | bytes 786436
  95.8 62.6 %collective-permute-start.9 = (f32[512,512]{1,0:T(8,128)S(1)}, f32[512,512]{1,0:T(8,128)S(1)}, u32[]{:S(2)}, u32[]{:S(2)}) collective-permute-start(f32[512,512]{1,0:T(8,128)S(1)} %copy.7), channel_id=1, source_target_pairs={{0,32},{8,40},{16,48},{24,56},{32,0},{40,8},{48,16},{56,24},{64,96... | collective-permute-start | bytes 3145736 | tf_op jit(solution)/shard_map/ppermute | solution.py:14
Sparse Core Ops, SparseCore 0:
  261.6 79.3 all-gather.2
where the time goes:
time: 353 us; the launch traced here: 352 us
  waiting for transfers between devices  168 us (48%)
  blocking collectives  99.3 us (28%)
  starting transfers between devices  44.3 us (13%)
  between operations  17.7 us (5%)
  matrix products  11.8 us (3%)
  local copies, waits for them, and re-layouts  5.63 us (2%)
  other arithmetic  5.07 us (1%)
    psum x1, blocking collectives, per_device(): lax.psum((jnp.sum(jnp.square(grad_rows.astype(jnp.float32))), jnp.sum(con...  99.3 us
    ppermute x10, waiting for transfers between devices, partner(): lax.ppermute(shard, axis, [(i, i ^ 1 << stride) for i in range(lax.axis_s...  88.9 us
    all_gather x1, waiting for transfers between devices, per_device(): update = lax.all_gather(scaled[None], 'dp', axis=1, tiled=True)  79.6 us
    ppermute x10, starting transfers between devices, partner(): lax.ppermute(shard, axis, [(i, i ^ 1 << stride) for i in range(lax.axis_s...  44.2 us
    dot_general x6, matrix products, precise_dot(): jnp.dot(left, right, precision=lax.Precision.HIGHEST, preferred_element_t...  9.31 us
  transfers between devices with their start and end apart: 11, of which 10 were waited for; matrix products, arithmetic and copies ran while one was open for 1% of the time, Pallas kernels for 0%

commit v1 on v0

v1 whole, which is shorter than its diff:
```python
import jax
import jax.numpy as jnp
from jax import lax
from jax.experimental import pallas as pl
from jax.experimental.pallas import tpu as pltpu
from jax.sharding import PartitionSpec as P

GROUP = 8
SLAB = 64
ORDER = 512
HALF = ORDER // 2

epsilon = 1e-06
decay_rate = 0.95


def flipped(value, axis, mask):
    return lax.ppermute(value, axis, [(i, i ^ mask) for i in range(lax.axis_size(axis))])


def dot(left, right, dims=((1,), (0,))):
    return lax.dot_general(left, right, (dims, ((), ())), preferred_element_type=jnp.float32)


def short(value):
    return value.astype(jnp.bfloat16)


def refresh_kernel(scalars, *refs):
    pieces = refs[:8]
    left_own, right_own, left_out, right_out, cond_out, sums_out = refs[8:14]
    grad, old_left, old_right, work, poly, total = refs[14:]
    member = scalars[0]
    for relative, piece in enumerate(pieces):
        rows = pl.ds(pl.multiple_of((member ^ relative) * SLAB, SLAB), SLAB)
        grad[rows, :] = piece[0:SLAB, :]
        old_left[rows, :] = piece[SLAB : 2 * SLAB, :]
        old_right[rows, :] = piece[2 * SLAB :, :]
    own = pl.ds(pl.multiple_of(member * SLAB, SLAB), SLAB)

    def start(old, own_old, out, dims):
        work[...] = dot(grad[...], grad[...], dims)
        out[...] = decay_rate * own_old[...] + work[own, :]
        factor = work[...] + decay_rate * old[...].astype(jnp.float32)
        scaling = 2.5 / jnp.sqrt(jnp.sum(factor * factor, keepdims=True) + epsilon)
        work[...] = factor * (scaling * 0.25)
        return jnp.sqrt(jnp.sqrt(scaling))

    def advance():
        quarter = work[...]
        low = short(quarter)
        poly[...] = 2.5 * quarter - dot(low, low)
        low_square = short(poly[...])
        fourth = 3.125 * poly[...] - dot(low_square, low_square)
        work[...] = 2.44140625 * quarter - dot(short(fourth), low)

    def apply_left():
        total[...] = 1.25 * total[...] - dot(short(work[...]), short(total[...]))

    def apply_right():
        total[...] = 1.25 * total[...] - dot(short(total[...]), short(work[...]))

    def chain(count, apply):
        apply()

        @pl.when(count > 1)
        def _():
            advance()
            apply()

        @pl.when(count > 2)
        def _():
            advance()
            apply()

    total[...] = grad[...].astype(jnp.float32)
    grad_square = jnp.sum(total[...] * total[...], keepdims=True)
    left_scale = start(old_left, left_own, left_out, ((1,), (1,)))
    chain(scalars[1], apply_left)
    right_scale = start(old_right, right_own, right_out, ((0,), (0,)))
    chain(scalars[2], apply_right)
    conditioned = total[...] * (left_scale * right_scale)
    cond_out[...] = short(conditioned)
    sums_out[0:4, :] = jnp.broadcast_to(jnp.sum(conditioned * conditioned, keepdims=True), (4, 128))
    sums_out[4:8, :] = jnp.broadcast_to(grad_square, (4, 128))


def refresh(scalars, pieces, left_own, right_own):
    vmem = pl.BlockSpec(memory_space=pltpu.VMEM)
    full = (ORDER, ORDER)
    return pl.pallas_call(
        refresh_kernel,
        out_shape=(
            jax.ShapeDtypeStruct((SLAB, ORDER), jnp.float32),
            jax.ShapeDtypeStruct((SLAB, ORDER), jnp.float32),
            jax.ShapeDtypeStruct(full, jnp.bfloat16),
            jax.ShapeDtypeStruct((8, 128), jnp.float32),
        ),
        in_specs=[pl.BlockSpec(memory_space=pltpu.SMEM)] + [vmem] * 10,
        out_specs=(vmem,) * 4,
        scratch_shapes=[pltpu.VMEM(full, jnp.bfloat16)] * 3 + [pltpu.VMEM(full, jnp.float32)] * 3,
        compiler_params=pltpu.CompilerParams(vmem_limit_bytes=40 * 1024 * 1024),
        name="refresh",
    )(scalars, *pieces, left_own, right_own)


def place_kernel(scalars, ratio, *refs):
    sources, out = refs[:4], refs[4]
    for relative, source in enumerate(sources):
        place = scalars[0] ^ relative
        rows = pl.ds(pl.multiple_of(place * HALF, HALF), HALF)
        out[rows, :] = short(source[0].astype(jnp.float32) * ratio[0:1, 0:1])


def place(scalars, ratio, sources):
    columns = 4
    piece = pl.BlockSpec((1, HALF, ORDER), lambda i: (i, 0, 0))
    return pl.pallas_call(
        place_kernel,
        out_shape=jax.ShapeDtypeStruct((columns * 2 * ORDER, ORDER), jnp.bfloat16),
        grid=(columns,),
        in_specs=[pl.BlockSpec(memory_space=pltpu.SMEM), pl.BlockSpec((8, 128), lambda i: (0, 0))]
        + [piece] * 4,
        out_specs=pl.BlockSpec((2 * ORDER, ORDER), lambda i: (i, 0)),
        compiler_params=pltpu.CompilerParams(vmem_limit_bytes=40 * 1024 * 1024),
        name="place",
    )(scalars, ratio, *sources)


def per_device(grads, left_old, right_old, root_steps):
    position = lax.axis_index("dp")
    member = position % GROUP
    block = position // GROUP
    core = position % 2
    own = jnp.concatenate([grads[0], short(left_old[0]), short(right_old[0])], axis=0)
    far = flipped(own, "dp", 4)
    near = flipped(own, "dp", 2)
    both = flipped(far, "dp", 2)
    pieces = [None] * 8
    for relative, piece in ((0, own), (2, near), (4, far), (6, both)):
        pieces[relative] = piece
        pieces[relative + 1] = flipped(piece, "dp", 1)
    counts = lax.dynamic_index_in_dim(root_steps[0], block, 0, keepdims=False)
    scalars = jnp.stack([member, counts[0], counts[1]])
    left_rows, right_rows, conditioned, sums = refresh(scalars, pieces, left_old[0], right_old[0])

    columns = [[16 * i + k for i in range(4)] for k in range(16)]

    def to_columns(value):
        copies = jnp.broadcast_to(value[None], (4, *value.shape))
        return lax.all_to_all(copies, "dp", 0, 0, axis_index_groups=columns)

    half = lax.dynamic_slice_in_dim(conditioned, core * HALF, HALF, 0)
    mirrored = flipped(half, "dp", 14)
    same = to_columns(half)
    cross = to_columns(mirrored)
    same_other = flipped(same, "dp", 1)
    cross_other = flipped(cross, "dp", 1)

    stacks = lax.all_to_all(jnp.broadcast_to(sums[None], (8, 8, 128)), "shard", 0, 0)
    sums = jnp.sum(stacks, axis=0)
    sums = sums + flipped(sums, "dp", 14)
    sums = jnp.sum(to_columns(sums), axis=0)
    ratio = jnp.sqrt(sums[4:5] / (sums[0:1] + epsilon))
    ratio = jnp.broadcast_to(ratio, (8, 128))

    slot = (block % 2) * 2 + core
    update = place(
        jnp.reshape(slot, (1,)), ratio, [same, same_other, cross, cross_other]
    )
    return (update[None], left_rows[None], right_rows[None])


def solution(mesh):
    placed = (
        P("shard", "dp", None),
        P("shard", "dp", None),
        P("shard", "dp", None),
        P("shard", None, None),
    )
    return jax.shard_map(
        per_device,
        mesh=mesh,
        in_specs=placed,
        out_specs=(P("shard", None, None), P("shard", "dp", None), P("shard", "dp", None)),
        check_vma=False,
    )
```

time: 353 us -> 124 us (0.35)
  the two profiles are of different devices: /device:TPU:1 before, /device:TPU:16 now
where the time goes in v1:
time: 124 us; the launch traced here: 123 us
  starting transfers between devices  50.6 us (41%)
  waiting for transfers between devices  32.9 us (27%)
  blocking collectives  22 us (18%)
  Pallas kernels  8.7 us (7%)
  local copies, waits for them, and re-layouts  5.15 us (4%)
  other arithmetic  3.24 us (3%)
    ppermute x11, starting transfers between devices, flipped(): lax.ppermute(value, axis, [(i, i ^ mask) for i in range(lax.axis_size(axi...  38.2 us
    all_to_all x1, blocking collectives, per_device(): lax.all_to_all(jnp.broadcast_to(sums[None], (8, 8, 128)), 'shard', 0, 0)  22 us
    all_to_all x3, waiting for transfers between devices, to_columns(): return lax.all_to_all(copies, 'dp', 0, 0, axis_index_groups=columns)  19.5 us
    ppermute x11, waiting for transfers between devices, flipped(): lax.ppermute(value, axis, [(i, i ^ mask) for i in range(lax.axis_size(axi...  13.4 us
    all_to_all x3, starting transfers between devices, to_columns(): return lax.all_to_all(copies, 'dp', 0, 0, axis_index_groups=columns)  12.4 us
    pallas_call x1, Pallas kernels, place(): pl.pallas_call(place_kernel, out_shape=jax.ShapeDtypeStruct((columns * 2...  4.53 us
    pallas_call x1, Pallas kernels, refresh(): pl.pallas_call(refresh_kernel, out_shape=(jax.ShapeDtypeStruct((SLAB, ORD...  4.17 us
    broadcast_in_dim x3, local copies, waits for them, and re-layouts, to_columns(): copies = jnp.broadcast_to(value[None], (4, *value.shape))  2.72 us
  transfers between devices with their start and end apart: 14, of which 6 were waited for; matrix products, arithmetic and copies ran while one was open for 2% of the time, Pallas kernels for 0%

profile of v1, /device:TPU:16, one launch (start us, length us, event | category | flops | bytes accessed | tf_op | source)
XLA Modules:
  0.0 123.5 jit_solution(18437635908576358641)
XLA Ops:
  0.6 0.0 copy-start
  0.6 1.0 bitcast_convert_fusion
  1.6 0.9 pad_maximum_fusion.refs_0_
  2.5 7.6 %collective-permute-start.3 = (bf16[192,512]{1,0:T(8,128)(2,1)S(1)}, bf16[192,512]{1,0:T(8,128)(2,1)S(1)}, u32[]{:S(2)}, u32[]{:S(2)}) collective-permute-start(bf16[192,512]{1,0:T(8,128)(2,1)S(1)} %pad_maximum_fusion.refs_0_), channel_id=1, source_target_pairs={{0,32},{8,40},{16,48},{24,56},{32,0},{40,8},{48,16},{56,24},{64,96... | collective-permute-start | bytes 589832 | tf_op jit(solution)/shard_map/ppermute | solution.py:18
  10.1 1.9 %collective-permute-start.1 = (bf16[192,512]{1,0:T(8,128)(2,1)S(1)}, bf16[192,512]{1,0:T(8,128)(2,1)S(1)}, u32[]{:S(2)}, u32[]{:S(2)}) collective-permute-start(bf16[192,512]{1,0:T(8,128)(2,1)S(1)} %pad_maximum_fusion.refs_0_), channel_id=1, source_target_pairs={{0,16},{8,24},{16,0},{24,8},{32,48},{40,56},{48,32},{56,40},{64,80... | collective-permute-start | bytes 589832 | tf_op jit(solution)/shard_map/ppermute | solution.py:18
  12.1 3.1 %collective-permute-done.3.refs_4_ = bf16[192,512]{1,0:T(8,128)(2,1)S(1)} collective-permute-done((bf16[192,512]{1,0:T(8,128)(2,1)S(1)}, bf16[192,512]{1,0:T(8,128)(2,1)S(1)}, u32[]{:S(2)}, u32[]{:S(2)}) %collective-permute-start.3) | collective-permute-done | bytes 196640 | tf_op jit(solution)/shard_map/ppermute | solution.py:18
  15.1 4.5 %collective-permute-start.5 = (bf16[192,512]{1,0:T(8,128)(2,1)S(1)}, bf16[192,512]{1,0:T(8,128)(2,1)S(1)}, u32[]{:S(2)}, u32[]{:S(2)}) collective-permute-start(bf16[192,512]{1,0:T(8,128)(2,1)S(1)} %collective-permute-done.3.refs_4_), channel_id=1, source_target_pairs={{0,16},{8,24},{16,0},{24,8},{32,48},{40,56},{48,32},{56,40},{64,80... | collective-permute-start | bytes 589832 | tf_op jit(solution)/shard_map/ppermute | solution.py:18
  19.7 1.9 %collective-permute-start = (bf16[192,512]{1,0:T(8,128)(2,1)S(1)}, bf16[192,512]{1,0:T(8,128)(2,1)S(1)}, u32[]{:S(2)}, u32[]{:S(2)}) collective-permute-start(bf16[192,512]{1,0:T(8,128)(2,1)S(1)} %pad_maximum_fusion.refs_0_), channel_id=1, source_target_pairs={{0,8},{8,0},{16,24},{24,16},{32,40},{40,32},{48,56},{56,48},{64,72... | collective-permute-start | bytes 589832 | tf_op jit(solution)/shard_map/ppermute | solution.py:18
  21.6 0.0 copy-done
  21.6 0.1 constant_dynamic-slice_fusion.1
  21.7 2.4 %collective-permute-start.4 = (bf16[192,512]{1,0:T(8,128)(2,1)S(1)}, bf16[192,512]{1,0:T(8,128)(2,1)S(1)}, u32[]{:S(2)}, u32[]{:S(2)}) collective-permute-start(bf16[192,512]{1,0:T(8,128)(2,1)S(1)} %collective-permute-done.3.refs_4_), channel_id=1, source_target_pairs={{0,8},{8,0},{16,24},{24,16},{32,40},{40,32},{48,56},{56,48},{64,72... | collective-permute-start | bytes 589832 | tf_op jit(solution)/shard_map/ppermute | solution.py:18
  24.1 0.0 collective-permute-done.1.refs_2_
  24.1 1.9 %collective-permute-start.2 = (bf16[192,512]{1,0:T(8,128)(2,1)S(1)}, bf16[192,512]{1,0:T(8,128)(2,1)S(1)}, u32[]{:S(2)}, u32[]{:S(2)}) collective-permute-start(bf16[192,512]{1,0:T(8,128)(2,1)S(1)} %collective-permute-done.1.refs_2_), channel_id=1, source_target_pairs={{0,8},{8,0},{16,24},{24,16},{32,40},{40,32},{48,56},{56,48},{64,72... | collective-permute-start | bytes 589832 | tf_op jit(solution)/shard_map/ppermute | solution.py:18
  26.1 0.0 collective-permute-done.5.refs_6_
  26.1 2.4 %collective-permute-start.6 = (bf16[192,512]{1,0:T(8,128)(2,1)S(1)}, bf16[192,512]{1,0:T(8,128)(2,1)S(1)}, u32[]{:S(2)}, u32[]{:S(2)}) collective-permute-start(bf16[192,512]{1,0:T(8,128)(2,1)S(1)} %collective-permute-done.5.refs_6_), channel_id=1, source_target_pairs={{0,8},{8,0},{16,24},{24,16},{32,40},{40,32},{48,56},{56,48},{64,72... | collective-permute-start | bytes 589832 | tf_op jit(solution)/shard_map/ppermute | solution.py:18
  28.5 0.5 fusion
  29.0 1.4 %pad_add_fusion.scalars = s32[3]{0:T(128)S(1)} fusion(s32[1]{0:T(128)} %bitcast.3, s32[1]{0:T(128)} %bitcast.2, s32[1]{0:T(128)} %bitcast.1), kind=kLoop, calls=%fused_computation.1 | loop fusion | flops 6 | bytes 24 | tf_op jit(solution)/shard_map/stack | solution.py:144
  30.4 0.0 collective-permute-done.refs_1_
  30.4 0.0 collective-permute-done.4.refs_5_
  30.4 0.0 collective-permute-done.2.refs_3_
  30.4 0.0 collective-permute-done.6.refs_7_
  30.4 0.0 copy-start.1
  30.4 0.9 copy-done.1
  31.3 0.0 copy-start.2
  31.3 0.9 copy-done.2
  32.2 4.2 %refresh.1 = (f32[64,512]{1,0:T(8,128)}, f32[64,512]{1,0:T(8,128)}, bf16[512,512]{1,0:T(8,128)(2,1)S(1)}, f32[8,128]{1,0:T(8,128)S(1)}) custom-call(s32[3]{0:T(128)S(1)} %pad_add_fusion.scalars, bf16[192,512]{1,0:T(8,128)(2,1)S(1)} %pad_maximum_fusion.refs_0_, bf16[192,512]{1,0:T(8,128)(2,1)S(1)} %collective-permute-done.refs_1_, ...), custom_call_target="tpu_custom_call" | custom-call | tf_op jit(solution)/shard_map/refresh/pallas_call | solution.py:91
  36.4 1.1 broadcast_in_dim.44
  37.5 5.6 %all-to-all-start.2 = ((bf16[4,256,512]{2,1,0:T(8,128)(2,1)}), bf16[4,256,512]{2,1,0:T(8,128)(2,1)S(1)}, u32[]{:S(2)}, u32[]{:S(2)}) async-start(bf16[4,256,512]{2,1,0:T(8,128)(2,1)} %broadcast_in_dim.44), calls=%async_computation.2 | async-start | bytes 2097152 | tf_op jit(solution)/shard_map/all_to_all | solution.py:151
  43.0 7.2 %collective-permute-start.9 = (bf16[256,512]{1,0:T(8,128)(2,1)S(1)}, bf16[256,512]{1,0:T(8,128)(2,1)S(1)}, u32[]{:S(2)}, u32[]{:S(2)}) collective-permute-start(bf16[256,512]{1,0:T(8,128)(2,1)S(1)} %constant_dynamic-slice_fusion), channel_id=1, source_target_pairs={{0,112},{8,120},{16,96},{24,104},{32,80},{40,88},{48,64},{56,72},{... | collective-permute-start | bytes 786440 | tf_op jit(solution)/shard_map/ppermute | solution.py:18
  50.2 6.3 %collective-permute-done.9 = bf16[256,512]{1,0:T(8,128)(2,1)S(1)} collective-permute-done((bf16[256,512]{1,0:T(8,128)(2,1)S(1)}, bf16[256,512]{1,0:T(8,128)(2,1)S(1)}, u32[]{:S(2)}, u32[]{:S(2)}) %collective-permute-start.9) | collective-permute-done | bytes 262176 | tf_op jit(solution)/shard_map/ppermute | solution.py:18
  56.5 1.8 %all-to-all-done.2.refs_0_ = bf16[4,256,512]{2,1,0:T(8,128)(2,1)S(1)} async-done(((bf16[4,256,512]{2,1,0:T(8,128)(2,1)}), bf16[4,256,512]{2,1,0:T(8,128)(2,1)S(1)}, u32[]{:S(2)}, u32[]{:S(2)}) %all-to-all-start.2) | async-done | bytes 1048608 | tf_op jit(solution)/shard_map/all_to_all | solution.py:151
  58.3 1.1 broadcast_in_dim.45
  59.4 3.5 %all-to-all-start.3 = ((bf16[4,256,512]{2,1,0:T(8,128)(2,1)}), bf16[4,256,512]{2,1,0:T(8,128)(2,1)S(1)}, u32[]{:S(2)}, u32[]{:S(2)}) async-start(bf16[4,256,512]{2,1,0:T(8,128)(2,1)} %broadcast_in_dim.45), calls=%async_computation.3 | async-start | bytes 2097152 | tf_op jit(solution)/shard_map/all_to_all | solution.py:151
  62.9 1.9 %collective-permute-start.8 = (bf16[4,256,512]{2,1,0:T(8,128)(2,1)S(1)}, bf16[4,256,512]{2,1,0:T(8,128)(2,1)S(1)}, u32[]{:S(2)}, u32[]{:S(2)}) collective-permute-start(bf16[4,256,512]{2,1,0:T(8,128)(2,1)S(1)} %all-to-all-done.2.refs_0_), channel_id=1, source_target_pairs={{0,8},{8,0},{16,24},{24,16},{32,40},{40,32},{48,56},{56,48},{64,72... | collective-permute-start | bytes 3145736 | tf_op jit(solution)/shard_map/ppermute | solution.py:18
  64.8 12.4 %all-to-all-done.3.refs_2_ = bf16[4,256,512]{2,1,0:T(8,128)(2,1)S(1)} async-done(((bf16[4,256,512]{2,1,0:T(8,128)(2,1)}), bf16[4,256,512]{2,1,0:T(8,128)(2,1)S(1)}, u32[]{:S(2)}, u32[]{:S(2)}) %all-to-all-start.3) | async-done | bytes 1048608 | tf_op jit(solution)/shard_map/all_to_all | solution.py:151
  77.2 1.9 %collective-permute-start.10 = (bf16[4,256,512]{2,1,0:T(8,128)(2,1)S(1)}, bf16[4,256,512]{2,1,0:T(8,128)(2,1)}, u32[]{:S(2)}, u32[]{:S(2)}) collective-permute-start(bf16[4,256,512]{2,1,0:T(8,128)(2,1)S(1)} %all-to-all-done.3.refs_2_), channel_id=1, source_target_pairs={{0,8},{8,0},{16,24},{24,16},{32,40},{40,32},{48,56},{56,48},{64,72... | collective-permute-start | bytes 3145736 | tf_op jit(solution)/shard_map/ppermute | solution.py:18
  79.2 22.0 %all_to_all.20 = f32[8,8,128]{2,1,0:T(8,128)S(1)} all-to-all(f32[8,8,128]{2,1,0:T(8,128)S(1)} %broadcast_in_dim.18), channel_id=1, replica_groups=mesh['dp'=64,'shard'=8] {'shard'}, dimensions={0} | all-to-all | bytes 65536 | tf_op jit(solution)/shard_map/all_to_all | solution.py:160
  101.2 4.5 %collective-permute-start.7 = (f32[8,128]{1,0:T(8,128)S(1)}, f32[8,128]{1,0:T(8,128)S(1)}, u32[]{:S(2)}, u32[]{:S(2)}) collective-permute-start(f32[8,128]{1,0:T(8,128)S(1)} %reduce_sum.18), channel_id=1, source_target_pairs={{0,112},{8,120},{16,96},{24,104},{32,80},{40,88},{48,64},{56,72},{... | collective-permute-start | bytes 12296 | tf_op jit(solution)/shard_map/ppermute | solution.py:18
  105.7 4.0 %collective-permute-done.7 = f32[8,128]{1,0:T(8,128)S(1)} collective-permute-done((f32[8,128]{1,0:T(8,128)S(1)}, f32[8,128]{1,0:T(8,128)S(1)}, u32[]{:S(2)}, u32[]{:S(2)}) %collective-permute-start.7) | collective-permute-done | bytes 4128 | tf_op jit(solution)/shard_map/ppermute | solution.py:18
  109.7 0.6 broadcast_in_dim.19
  110.3 3.3 %all-to-all-start.1 = ((f32[4,8,128]{2,1,0:T(8,128)}), f32[4,8,128]{2,1,0:T(8,128)S(1)}, u32[]{:S(2)}, u32[]{:S(2)}) async-start(f32[4,8,128]{2,1,0:T(8,128)} %broadcast_in_dim.19), calls=%async_computation.1 | async-start | bytes 32768 | tf_op jit(solution)/shard_map/all_to_all | solution.py:151
  113.6 5.3 %all-to-all-done.1 = f32[4,8,128]{2,1,0:T(8,128)S(1)} async-done(((f32[4,8,128]{2,1,0:T(8,128)}), f32[4,8,128]{2,1,0:T(8,128)S(1)}, u32[]{:S(2)}, u32[]{:S(2)}) %all-to-all-start.1) | async-done | bytes 16416 | tf_op jit(solution)/shard_map/all_to_all | solution.py:151
  118.9 0.0 collective-permute-done.8.refs_1_
  118.9 0.0 collective-permute-done.10.refs_3_
  118.9 4.5 %place.1 = bf16[4096,512]{1,0:T(8,128)(2,1)} custom-call(s32[1]{0:T(128)} %bitcast.scalars, f32[8,128]{1,0:T(8,128)S(1)} %broadcast_in_dim.21.ratio, bf16[4,256,512]{2,1,0:T(8,128)(2,1)S(1)} %all-to-all-done.2.refs_0_, bf16[4,256,512]{2,1,0:T(8,128)(2,1)S(1)} %collective-permute-done.8.refs_1_, bf16[4,256,512]{2,1,0:T(8,128)(2,1)S(1)} %all-to-all-done.3.refs_2_, ...), custom_call_target="tpu_custom_call" | custom-call | tf_op jit(solution)/shard_map/place/pallas_call | solution.py:118
  (7 shorter events, 0.1 us)
Async XLA Ops:
  0.6 21.0 %copy-start = (s32[1,8,2]{1,2,0:T(2,128)S(1)}, s32[1,8,2]{1,2,0:T(2,128)}, u32[]{:S(2)}) copy-start(s32[1,8,2]{1,2,0:T(2,128)} %param.7) | copy-start | bytes 196
  2.5 12.7 %collective-permute-start.3 = (bf16[192,512]{1,0:T(8,128)(2,1)S(1)}, bf16[192,512]{1,0:T(8,128)(2,1)S(1)}, u32[]{:S(2)}, u32[]{:S(2)}) collective-permute-start(bf16[192,512]{1,0:T(8,128)(2,1)S(1)} %pad_maximum_fusion.refs_0_), channel_id=1, source_target_pairs={{0,32},{8,40},{16,48},{24,56},{32,0},{40,8},{48,16},{56,24},{64,96... | collective-permute-start | bytes 589832 | tf_op jit(solution)/shard_map/ppermute | solution.py:18
  10.1 14.0 %collective-permute-start.1 = (bf16[192,512]{1,0:T(8,128)(2,1)S(1)}, bf16[192,512]{1,0:T(8,128)(2,1)S(1)}, u32[]{:S(2)}, u32[]{:S(2)}) collective-permute-start(bf16[192,512]{1,0:T(8,128)(2,1)S(1)} %pad_maximum_fusion.refs_0_), channel_id=1, source_target_pairs={{0,16},{8,24},{16,0},{24,8},{32,48},{40,56},{48,32},{56,40},{64,80... | collective-permute-start | bytes 589832 | tf_op jit(solution)/shard_map/ppermute | solution.py:18
  15.1 10.9 %collective-permute-start.5 = (bf16[192,512]{1,0:T(8,128)(2,1)S(1)}, bf16[192,512]{1,0:T(8,128)(2,1)S(1)}, u32[]{:S(2)}, u32[]{:S(2)}) collective-permute-start(bf16[192,512]{1,0:T(8,128)(2,1)S(1)} %collective-permute-done.3.refs_4_), channel_id=1, source_target_pairs={{0,16},{8,24},{16,0},{24,8},{32,48},{40,56},{48,32},{56,40},{64,80... | collective-permute-start | bytes 589832 | tf_op jit(solution)/shard_map/ppermute | solution.py:18
  19.7 10.7 %collective-permute-start = (bf16[192,512]{1,0:T(8,128)(2,1)S(1)}, bf16[192,512]{1,0:T(8,128)(2,1)S(1)}, u32[]{:S(2)}, u32[]{:S(2)}) collective-permute-start(bf16[192,512]{1,0:T(8,128)(2,1)S(1)} %pad_maximum_fusion.refs_0_), channel_id=1, source_target_pairs={{0,8},{8,0},{16,24},{24,16},{32,40},{40,32},{48,56},{56,48},{64,72... | collective-permute-start | bytes 589832 | tf_op jit(solution)/shard_map/ppermute | solution.py:18
  21.7 8.7 %collective-permute-start.4 = (bf16[192,512]{1,0:T(8,128)(2,1)S(1)}, bf16[192,512]{1,0:T(8,128)(2,1)S(1)}, u32[]{:S(2)}, u32[]{:S(2)}) collective-permute-start(bf16[192,512]{1,0:T(8,128)(2,1)S(1)} %collective-permute-done.3.refs_4_), channel_id=1, source_target_pairs={{0,8},{8,0},{16,24},{24,16},{32,40},{40,32},{48,56},{56,48},{64,72... | collective-permute-start | bytes 589832 | tf_op jit(solution)/shard_map/ppermute | solution.py:18
  24.1 6.2 %collective-permute-start.2 = (bf16[192,512]{1,0:T(8,128)(2,1)S(1)}, bf16[192,512]{1,0:T(8,128)(2,1)S(1)}, u32[]{:S(2)}, u32[]{:S(2)}) collective-permute-start(bf16[192,512]{1,0:T(8,128)(2,1)S(1)} %collective-permute-done.1.refs_2_), channel_id=1, source_target_pairs={{0,8},{8,0},{16,24},{24,16},{32,40},{40,32},{48,56},{56,48},{64,72... | collective-permute-start | bytes 589832 | tf_op jit(solution)/shard_map/ppermute | solution.py:18
  26.1 4.3 %collective-permute-start.6 = (bf16[192,512]{1,0:T(8,128)(2,1)S(1)}, bf16[192,512]{1,0:T(8,128)(2,1)S(1)}, u32[]{:S(2)}, u32[]{:S(2)}) collective-permute-start(bf16[192,512]{1,0:T(8,128)(2,1)S(1)} %collective-permute-done.5.refs_6_), channel_id=1, source_target_pairs={{0,8},{8,0},{16,24},{24,16},{32,40},{40,32},{48,56},{56,48},{64,72... | collective-permute-start | bytes 589832 | tf_op jit(solution)/shard_map/ppermute | solution.py:18
  30.4 0.9 copy-start.1
  31.3 0.9 copy-start.2
  37.5 20.9 %all-to-all-start.2 = ((bf16[4,256,512]{2,1,0:T(8,128)(2,1)}), bf16[4,256,512]{2,1,0:T(8,128)(2,1)S(1)}, u32[]{:S(2)}, u32[]{:S(2)}) async-start(bf16[4,256,512]{2,1,0:T(8,128)(2,1)} %broadcast_in_dim.44), calls=%async_computation.2 | async-start | bytes 2097152 | tf_op jit(solution)/shard_map/all_to_all | solution.py:151
  43.0 13.5 %collective-permute-start.9 = (bf16[256,512]{1,0:T(8,128)(2,1)S(1)}, bf16[256,512]{1,0:T(8,128)(2,1)S(1)}, u32[]{:S(2)}, u32[]{:S(2)}) collective-permute-start(bf16[256,512]{1,0:T(8,128)(2,1)S(1)} %constant_dynamic-slice_fusion), channel_id=1, source_target_pairs={{0,112},{8,120},{16,96},{24,104},{32,80},{40,88},{48,64},{56,72},{... | collective-permute-start | bytes 786440 | tf_op jit(solution)/shard_map/ppermute | solution.py:18
  59.4 17.9 %all-to-all-start.3 = ((bf16[4,256,512]{2,1,0:T(8,128)(2,1)}), bf16[4,256,512]{2,1,0:T(8,128)(2,1)S(1)}, u32[]{:S(2)}, u32[]{:S(2)}) async-start(bf16[4,256,512]{2,1,0:T(8,128)(2,1)} %broadcast_in_dim.45), calls=%async_computation.3 | async-start | bytes 2097152 | tf_op jit(solution)/shard_map/all_to_all | solution.py:151
  62.9 56.0 %collective-permute-start.8 = (bf16[4,256,512]{2,1,0:T(8,128)(2,1)S(1)}, bf16[4,256,512]{2,1,0:T(8,128)(2,1)S(1)}, u32[]{:S(2)}, u32[]{:S(2)}) collective-permute-start(bf16[4,256,512]{2,1,0:T(8,128)(2,1)S(1)} %all-to-all-done.2.refs_0_), channel_id=1, source_target_pairs={{0,8},{8,0},{16,24},{24,16},{32,40},{40,32},{48,56},{56,48},{64,72... | collective-permute-start | bytes 3145736 | tf_op jit(solution)/shard_map/ppermute | solution.py:18
  77.2 41.7 %collective-permute-start.10 = (bf16[4,256,512]{2,1,0:T(8,128)(2,1)S(1)}, bf16[4,256,512]{2,1,0:T(8,128)(2,1)}, u32[]{:S(2)}, u32[]{:S(2)}) collective-permute-start(bf16[4,256,512]{2,1,0:T(8,128)(2,1)S(1)} %all-to-all-done.3.refs_2_), channel_id=1, source_target_pairs={{0,8},{8,0},{16,24},{24,16},{32,40},{40,32},{48,56},{56,48},{64,72... | collective-permute-start | bytes 3145736 | tf_op jit(solution)/shard_map/ppermute | solution.py:18
  101.2 8.5 %collective-permute-start.7 = (f32[8,128]{1,0:T(8,128)S(1)}, f32[8,128]{1,0:T(8,128)S(1)}, u32[]{:S(2)}, u32[]{:S(2)}) collective-permute-start(f32[8,128]{1,0:T(8,128)S(1)} %reduce_sum.18), channel_id=1, source_target_pairs={{0,112},{8,120},{16,96},{24,104},{32,80},{40,88},{48,64},{56,72},{... | collective-permute-start | bytes 12296 | tf_op jit(solution)/shard_map/ppermute | solution.py:18
  110.3 8.6 %all-to-all-start.1 = ((f32[4,8,128]{2,1,0:T(8,128)}), f32[4,8,128]{2,1,0:T(8,128)S(1)}, u32[]{:S(2)}, u32[]{:S(2)}) async-start(f32[4,8,128]{2,1,0:T(8,128)} %broadcast_in_dim.19), calls=%async_computation.1 | async-start | bytes 32768 | tf_op jit(solution)/shard_map/all_to_all | solution.py:151

commit v2 on v1

v2 whole, which is shorter than its diff:
```python
import jax
import jax.numpy as jnp
from jax import lax
from jax.experimental import pallas as pl
from jax.experimental.pallas import tpu as pltpu
from jax.sharding import PartitionSpec as P

GROUP = 8
SLAB = 64
ORDER = 512
HALF = ORDER // 2
SENT = HALF + 16
PANEL = 256
COLUMNS = 4

epsilon = 1e-06
decay_rate = 0.95

VMEM = pl.BlockSpec(memory_space=pltpu.VMEM)
SMEM = pl.BlockSpec(memory_space=pltpu.SMEM)
HBM = pl.BlockSpec(memory_space=pltpu.HBM)
PARAMS = pltpu.CompilerParams(vmem_limit_bytes=16 * 1024 * 1024)


def flipped(value, axis, mask):
    return lax.ppermute(value, axis, [(i, i ^ mask) for i in range(lax.axis_size(axis))])


def dot(left, right, dims=((1,), (0,))):
    return lax.dot_general(left, right, (dims, ((), ())), preferred_element_type=jnp.float32)


def short(value):
    return value.astype(jnp.bfloat16)


def thirds(value):
    parts = []
    for _ in range(3):
        parts.append(jnp.broadcast_to(short(value), (1, ORDER)))
        value = value - short(value).astype(jnp.float32)
    return parts


def refresh_kernel(position, steps, *refs):
    pieces = refs[:8]
    products_out, half_out, copies_out = refs[8:11]
    grad, old_left, old_right, low, low_square, fourth, short_total, work, poly, total = refs[11:]
    member = position[0] & (GROUP - 1)
    block = position[0] // GROUP
    for relative, piece in enumerate(pieces):
        rows = pl.ds(pl.multiple_of((member ^ relative) * SLAB, SLAB), SLAB)
        grad[rows, :] = piece[0:SLAB, :]
        old_left[rows, :] = piece[SLAB : 2 * SLAB, :]
        old_right[rows, :] = piece[2 * SLAB :, :]
    own = pl.ds(pl.multiple_of(member * SLAB, SLAB), SLAB)

    panels = [pl.ds(row, PANEL) for row in range(0, ORDER, PANEL)]

    def start(side, old, dims):
        square = jnp.zeros((1, 1), jnp.float32)
        for rows in panels:
            if side == 0:
                product = dot(grad[rows, :], grad[...], dims)
            else:
                product = dot(grad[:, rows], grad[...], dims)
            work[rows, :] = product
            factor = product + decay_rate * old[rows, :].astype(jnp.float32)
            poly[rows, :] = factor
            square = square + jnp.sum(factor * factor, keepdims=True)
        products_out[side] = work[own, :]
        scaling = 2.5 / jnp.sqrt(square + epsilon)
        for rows in panels:
            quarter = poly[rows, :] * (scaling * 0.25)
            work[rows, :] = quarter
            low[rows, :] = short(quarter)
        return jnp.sqrt(jnp.sqrt(scaling))

    def advance():
        for rows in panels:
            partial = 2.5 * work[rows, :] - dot(low[rows, :], low[...])
            poly[rows, :] = partial
            low_square[rows, :] = short(partial)
        for rows in panels:
            fourth[rows, :] = short(
                3.125 * poly[rows, :] - dot(low_square[rows, :], low_square[...])
            )
        for rows in panels:
            work[rows, :] = 2.44140625 * work[rows, :] - dot(fourth[rows, :], low[...])
        for rows in panels:
            low[rows, :] = short(work[rows, :])

    def apply_left():
        for rows in panels:
            total[rows, :] = 1.25 * total[rows, :] - dot(low[rows, :], short_total[...])
        for rows in panels:
            short_total[rows, :] = short(total[rows, :])

    def apply_right():
        for rows in panels:
            value = 1.25 * total[rows, :] - dot(short_total[rows, :], low[...])
            total[rows, :] = value
            short_total[rows, :] = short(value)

    def chain(count, apply):
        apply()

        @pl.when(count > 1)
        def _():
            advance()
            apply()

        @pl.when(count > 2)
        def _():
            advance()
            apply()

    left_scale = start(0, old_left, ((1,), (1,)))
    grad_square = jnp.zeros((1, 1), jnp.float32)
    for rows in panels:
        value = grad[rows, :].astype(jnp.float32)
        total[rows, :] = value
        grad_square = grad_square + jnp.sum(value * value, keepdims=True)
        short_total[rows, :] = grad[rows, :]
    chain(steps[2 * block], apply_left)
    right_scale = start(1, old_right, ((0,), (0,)))
    chain(steps[2 * block + 1], apply_right)
    cond_square = jnp.zeros((1, 1), jnp.float32)
    for rows in panels:
        value = total[rows, :] * (left_scale * right_scale)
        total[rows, :] = value
        cond_square = cond_square + jnp.sum(value * value, keepdims=True)
    half = short(total[pl.ds(pl.multiple_of((member & 1) * HALF, HALF), HALF), :])
    half_out[0:HALF, :] = half
    half_out[HALF:, :] = jnp.concatenate(
        thirds(cond_square) + thirds(grad_square) + [jnp.zeros((10, ORDER), jnp.bfloat16)], axis=0
    )
    for column in range(COLUMNS):
        copies_out[column] = half_out[...]


def refresh(position, steps, pieces):
    full = (ORDER, ORDER)
    return pl.pallas_call(
        refresh_kernel,
        out_shape=(
            jax.ShapeDtypeStruct((2, SLAB, ORDER), jnp.float32),
            jax.ShapeDtypeStruct((SENT, ORDER), jnp.bfloat16),
            jax.ShapeDtypeStruct((COLUMNS, SENT, ORDER), jnp.bfloat16),
        ),
        in_specs=[SMEM] * 2 + [VMEM] * 8,
        out_specs=(VMEM,) * 3,
        scratch_shapes=[pltpu.VMEM(full, jnp.bfloat16)] * 7 + [pltpu.VMEM(full, jnp.float32)] * 3,
        compiler_params=PARAMS,
        name="refresh",
    )(position, steps, *pieces)


def spread_kernel(half, out):
    for column in range(COLUMNS):
        out[column] = half[...]


def spread(half):
    return pl.pallas_call(
        spread_kernel,
        out_shape=jax.ShapeDtypeStruct((COLUMNS, *half.shape), half.dtype),
        in_specs=[VMEM],
        out_specs=VMEM,
        compiler_params=PARAMS,
        name="spread",
    )(half)


def place_kernel(position, sums, *refs):
    sources, out, staged, sems = refs[:4], refs[4], refs[5], refs[6]
    squares = [sums[i : i + 1] + sums[i + 1 : i + 2] + sums[i + 2 : i + 3] for i in (0, 3)]
    ratio = jnp.sqrt(squares[1] / (squares[0] + epsilon))[:, 0:1]
    slot = ((position[0] // GROUP) & 1) * 2 + (position[0] & 1)
    stores = []
    for relative, source in enumerate(sources):
        for column in range(COLUMNS):
            index = relative * COLUMNS + column
            staged[index] = short(source[column, 0:HALF].astype(jnp.float32) * ratio)
            row = (column * 4 + (slot ^ relative)) * HALF
            rows = pl.ds(pl.multiple_of(row, HALF), HALF)
            store = pltpu.make_async_copy(staged.at[index], out.at[0, rows], sems.at[index])
            store.start()
            stores.append(store)
    for store in stores:
        store.wait()


def place(position, sums, sources):
    return pl.pallas_call(
        place_kernel,
        out_shape=jax.ShapeDtypeStruct((1, 4 * COLUMNS * HALF, ORDER), jnp.bfloat16),
        in_specs=[SMEM] + [VMEM] * 5,
        out_specs=HBM,
        scratch_shapes=[
            pltpu.VMEM((4 * COLUMNS, HALF, ORDER), jnp.bfloat16),
            pltpu.SemaphoreType.DMA((4 * COLUMNS,)),
        ],
        compiler_params=PARAMS,
        name="place",
    )(position, sums, *sources)


def tally(blocks):
    return jnp.sum(blocks[:, HALF : HALF + 8, 0:128].astype(jnp.float32), axis=0)


def per_device(grads, left_old, right_old, root_steps):
    position = jnp.reshape(lax.axis_index("dp"), (1,))
    steps = jnp.reshape(root_steps, (16,))
    own = short(jnp.concatenate([grads[0].astype(jnp.float32), left_old[0], right_old[0]], axis=0))
    far = flipped(own, "dp", 4)
    near = flipped(own, "dp", 2)
    far, steps = lax.optimization_barrier((far, steps))
    both = flipped(far, "dp", 2)
    pieces = [None] * 8
    for relative, piece in ((0, own), (2, near), (4, far), (6, both)):
        pieces[relative] = piece
        pieces[relative + 1] = flipped(piece, "dp", 1)
    products, half, copies = refresh(position, steps, pieces)
    left_rows = decay_rate * left_old + products[0:1]
    right_rows = decay_rate * right_old + products[1:2]

    columns = [[16 * i + k for i in range(COLUMNS)] for k in range(16)]
    mirrored = flipped(half, "dp", 14)
    same = lax.all_to_all(copies, "dp", 0, 0, axis_index_groups=columns)
    sums = tally(same)
    sums = sums + flipped(sums, "shard", 1)
    mirrored, sums, left_rows, right_rows = lax.optimization_barrier(
        (mirrored, sums, left_rows, right_rows)
    )
    mirrored = spread(mirrored)
    cross = lax.all_to_all(mirrored, "dp", 0, 0, axis_index_groups=columns)
    same_other = flipped(same, "dp", 1)
    for mask in (7, 2):
        sums = sums + flipped(sums, "shard", mask)
    cross, sums = lax.optimization_barrier((cross, sums))
    cross_other = flipped(cross, "dp", 1)
    sums = sums + flipped(sums, "dp", 14)
    update = place(position, sums, [same, same_other, cross, cross_other])
    return (update, left_rows, right_rows)


def solution(mesh):
    placed = (
        P("shard", "dp", None),
        P("shard", "dp", None),
        P("shard", "dp", None),
        P("shard", None, None),
    )
    return jax.shard_map(
        per_device,
        mesh=mesh,
        in_specs=placed,
        out_specs=(P("shard", None, None), P("shard", "dp", None), P("shard", "dp", None)),
        check_vma=False,
    )
```

time: 124 us -> 101 us (0.81)
  the two profiles are of different devices: /device:TPU:16 before, /device:TPU:18 now
where the time goes in v2:
time: 101 us; the launch traced here: 99.9 us
  starting transfers between devices  59.7 us (59%)
  waiting for transfers between devices  22.7 us (22%)
  Pallas kernels  13.2 us (13%)
  other arithmetic  2.6 us (3%)
    ppermute x14, starting transfers between devices, flipped(): lax.ppermute(value, axis, [(i, i ^ mask) for i in range(lax.axis_size(axi...  51.1 us
    ppermute x14, waiting for transfers between devices, flipped(): lax.ppermute(value, axis, [(i, i ^ mask) for i in range(lax.axis_size(axi...  12 us
    all_to_all x1, waiting for transfers between devices, per_device(): same = lax.all_to_all(copies, 'dp', 0, 0, axis_index_groups=columns)  10.7 us
    pallas_call x1, Pallas kernels, refresh(): pl.pallas_call(refresh_kernel, out_shape=(jax.ShapeDtypeStruct((2, SLAB,...  9.92 us
    all_to_all x1, starting transfers between devices, per_device(): cross = lax.all_to_all(mirrored, 'dp', 0, 0, axis_index_groups=columns)  4.95 us
    all_to_all x1, starting transfers between devices, per_device(): same = lax.all_to_all(copies, 'dp', 0, 0, axis_index_groups=columns)  3.64 us
    pallas_call x1, Pallas kernels, place(): pl.pallas_call(place_kernel, out_shape=jax.ShapeDtypeStruct((1, 4 * COLUM...  2.25 us
  transfers between devices with their start and end apart: 16, of which 7 were waited for; matrix products, arithmetic and copies ran while one was open for 2% of the time, Pallas kernels for 0%

profile of v2, /device:TPU:18, one launch (start us, length us, event | category | flops | bytes accessed | tf_op | source)
XLA Modules:
  0.0 99.9 jit_solution(7129960198088979500)
XLA Ops:
  0.6 1.0 convert_bitcast_fusion
  1.6 0.9 pad_maximum_fusion.refs_0_
  2.5 2.2 %collective-permute-start = (bf16[192,512]{1,0:T(8,128)(2,1)S(1)}, bf16[192,512]{1,0:T(8,128)(2,1)S(1)}, u32[]{:S(2)}, u32[]{:S(2)}) collective-permute-start(bf16[192,512]{1,0:T(8,128)(2,1)S(1)} %pad_maximum_fusion.refs_0_), channel_id=1, source_target_pairs={{0,32},{8,40},{16,48},{24,56},{32,0},{40,8},{48,16},{56,24},{64,96... | collective-permute-start | bytes 589832 | tf_op jit(solution)/shard_map/ppermute | solution.py:26
  4.7 3.5 %collective-permute-start.2 = (bf16[192,512]{1,0:T(8,128)(2,1)S(1)}, bf16[192,512]{1,0:T(8,128)(2,1)S(1)}, u32[]{:S(2)}, u32[]{:S(2)}) collective-permute-start(bf16[192,512]{1,0:T(8,128)(2,1)S(1)} %pad_maximum_fusion.refs_0_), channel_id=1, source_target_pairs={{0,16},{8,24},{16,0},{24,8},{32,48},{40,56},{48,32},{56,40},{64,80... | collective-permute-start | bytes 589832 | tf_op jit(solution)/shard_map/ppermute | solution.py:26
  8.2 0.8 copy.8
  9.0 0.1 reshape.15.steps
  9.1 4.1 %collective-permute-done.refs_4_ = bf16[192,512]{1,0:T(8,128)(2,1)S(1)} collective-permute-done((bf16[192,512]{1,0:T(8,128)(2,1)S(1)}, bf16[192,512]{1,0:T(8,128)(2,1)S(1)}, u32[]{:S(2)}, u32[]{:S(2)}) %collective-permute-start) | collective-permute-done | bytes 196640 | tf_op jit(solution)/shard_map/ppermute | solution.py:26
  13.1 6.5 %collective-permute-start.5 = (bf16[192,512]{1,0:T(8,128)(2,1)S(1)}, bf16[192,512]{1,0:T(8,128)(2,1)S(1)}, u32[]{:S(2)}, u32[]{:S(2)}) collective-permute-start(bf16[192,512]{1,0:T(8,128)(2,1)S(1)} %collective-permute-done.refs_4_), channel_id=1, source_target_pairs={{0,16},{8,24},{16,0},{24,8},{32,48},{40,56},{48,32},{56,40},{64,80... | collective-permute-start | bytes 589832 | tf_op jit(solution)/shard_map/ppermute | solution.py:26
  19.6 1.9 %collective-permute-start.1 = (bf16[192,512]{1,0:T(8,128)(2,1)S(1)}, bf16[192,512]{1,0:T(8,128)(2,1)S(1)}, u32[]{:S(2)}, u32[]{:S(2)}) collective-permute-start(bf16[192,512]{1,0:T(8,128)(2,1)S(1)} %pad_maximum_fusion.refs_0_), channel_id=1, source_target_pairs={{0,8},{8,0},{16,24},{24,16},{32,40},{40,32},{48,56},{56,48},{64,72... | collective-permute-start | bytes 589832 | tf_op jit(solution)/shard_map/ppermute | solution.py:26
  21.5 2.4 %collective-permute-start.4 = (bf16[192,512]{1,0:T(8,128)(2,1)S(1)}, bf16[192,512]{1,0:T(8,128)(2,1)S(1)}, u32[]{:S(2)}, u32[]{:S(2)}) collective-permute-start(bf16[192,512]{1,0:T(8,128)(2,1)S(1)} %collective-permute-done.refs_4_), channel_id=1, source_target_pairs={{0,8},{8,0},{16,24},{24,16},{32,40},{40,32},{48,56},{56,48},{64,72... | collective-permute-start | bytes 589832 | tf_op jit(solution)/shard_map/ppermute | solution.py:26
  23.9 0.0 collective-permute-done.2.refs_2_
  24.0 1.9 %collective-permute-start.3 = (bf16[192,512]{1,0:T(8,128)(2,1)S(1)}, bf16[192,512]{1,0:T(8,128)(2,1)S(1)}, u32[]{:S(2)}, u32[]{:S(2)}) collective-permute-start(bf16[192,512]{1,0:T(8,128)(2,1)S(1)} %collective-permute-done.2.refs_2_), channel_id=1, source_target_pairs={{0,8},{8,0},{16,24},{24,16},{32,40},{40,32},{48,56},{56,48},{64,72... | collective-permute-start | bytes 589832 | tf_op jit(solution)/shard_map/ppermute | solution.py:26
  25.9 0.0 collective-permute-done.5.refs_6_
  25.9 2.4 %collective-permute-start.6 = (bf16[192,512]{1,0:T(8,128)(2,1)S(1)}, bf16[192,512]{1,0:T(8,128)(2,1)S(1)}, u32[]{:S(2)}, u32[]{:S(2)}) collective-permute-start(bf16[192,512]{1,0:T(8,128)(2,1)S(1)} %collective-permute-done.5.refs_6_), channel_id=1, source_target_pairs={{0,8},{8,0},{16,24},{24,16},{32,40},{40,32},{48,56},{56,48},{64,72... | collective-permute-start | bytes 589832 | tf_op jit(solution)/shard_map/ppermute | solution.py:26
  28.3 0.0 collective-permute-done.1.refs_1_
  28.3 0.0 collective-permute-done.3.refs_3_
  28.3 0.0 collective-permute-done.4.refs_5_
  28.3 1.0 %collective-permute-done.6.refs_7_ = bf16[192,512]{1,0:T(8,128)(2,1)S(1)} collective-permute-done((bf16[192,512]{1,0:T(8,128)(2,1)S(1)}, bf16[192,512]{1,0:T(8,128)(2,1)S(1)}, u32[]{:S(2)}, u32[]{:S(2)}) %collective-permute-start.6) | collective-permute-done | bytes 196640 | tf_op jit(solution)/shard_map/ppermute | solution.py:26
  29.4 9.9 %refresh.1 = (f32[2,64,512]{2,1,0:T(8,128)S(1)}, bf16[272,512]{1,0:T(8,128)(2,1)S(1)}, bf16[4,272,512]{2,1,0:T(8,128)(2,1)}) custom-call(s32[1]{0:T(128)} %bitcast.position, s32[16]{0:T(128)S(1)} %reshape.15.steps, bf16[192,512]{1,0:T(8,128)(2,1)S(1)} %pad_maximum_fusion.refs_0_, bf16[192,512]{1,0:T(8,128)(2,1)S(1)} %collective-permute-done.1.refs_1_, ...), custom_call_target="tpu_custom_call" | custom-call | tf_op jit(solution)/shard_map/refresh/pallas_call | solution.py:144
  39.3 0.0 copy-start
  39.3 0.0 copy-start.1
  39.3 3.6 %all-to-all-start = ((bf16[4,272,512]{2,1,0:T(8,128)(2,1)}), bf16[4,272,512]{2,1,0:T(8,128)(2,1)S(1)}, u32[]{:S(2)}, u32[]{:S(2)}) async-start(bf16[4,272,512]{2,1,0:T(8,128)(2,1)} %get-tuple-element.17), calls=%async_computation | async-start | bytes 2228224 | tf_op jit(solution)/shard_map/all_to_all | solution.py:231
  42.9 4.0 %collective-permute-start.7 = (bf16[272,512]{1,0:T(8,128)(2,1)S(1)}, bf16[272,512]{1,0:T(8,128)(2,1)S(1)}, u32[]{:S(2)}, u32[]{:S(2)}) collective-permute-start(bf16[272,512]{1,0:T(8,128)(2,1)S(1)} %get-tuple-element.16), channel_id=1, source_target_pairs={{0,112},{8,120},{16,96},{24,104},{32,80},{40,88},{48,64},{56,72},{... | collective-permute-start | bytes 835592 | tf_op jit(solution)/shard_map/ppermute | solution.py:26
  46.9 10.7 %all-to-all-done.refs_0_ = bf16[4,272,512]{2,1,0:T(8,128)(2,1)S(1)} async-done(((bf16[4,272,512]{2,1,0:T(8,128)(2,1)}), bf16[4,272,512]{2,1,0:T(8,128)(2,1)S(1)}, u32[]{:S(2)}, u32[]{:S(2)}) %all-to-all-start) | async-done | bytes 1114144 | tf_op jit(solution)/shard_map/all_to_all | solution.py:231
  57.6 2.7 %collective-permute-start.8 = (f32[8,128]{1,0:T(8,128)S(1)}, f32[8,128]{1,0:T(8,128)S(1)}, u32[]{:S(2)}, u32[]{:S(2)}) collective-permute-start(f32[8,128]{1,0:T(8,128)S(1)} %convert_reduce_fusion), channel_id=1, source_target_pairs={{0,1},{1,0},{2,3},{3,2},{4,5},{5,4},{6,7},{7,6},{8,9},{9,8},{10,11... | collective-permute-start | bytes 12296 | tf_op jit(solution)/shard_map/ppermute | solution.py:26
  60.3 0.0 copy-done
  60.3 0.0 copy-done.1
  60.3 0.7 slice_add_fusion
  61.0 2.1 %collective-permute-done.8 = f32[8,128]{1,0:T(8,128)S(1)} collective-permute-done((f32[8,128]{1,0:T(8,128)S(1)}, f32[8,128]{1,0:T(8,128)S(1)}, u32[]{:S(2)}, u32[]{:S(2)}) %collective-permute-start.8) | collective-permute-done | bytes 4128 | tf_op jit(solution)/shard_map/ppermute | solution.py:26
  63.1 0.0 collective-permute-done.7.half
  63.1 1.1 %spread.1 = bf16[4,272,512]{2,1,0:T(8,128)(2,1)} custom-call(bf16[272,512]{1,0:T(8,128)(2,1)S(1)} %collective-permute-done.7.half), custom_call_target="tpu_custom_call" | custom-call | tf_op jit(solution)/shard_map/spread/pallas_call | solution.py:165
  64.2 5.0 %all-to-all-start.1 = ((bf16[4,272,512]{2,1,0:T(8,128)(2,1)}), bf16[4,272,512]{2,1,0:T(8,128)(2,1)S(1)}, u32[]{:S(2)}, u32[]{:S(2)}) async-start(bf16[4,272,512]{2,1,0:T(8,128)(2,1)} %spread.1), calls=%async_computation.1 | async-start | bytes 2228224 | tf_op jit(solution)/shard_map/all_to_all | solution.py:238
  69.1 9.8 %collective-permute-start.9 = (f32[8,128]{1,0:T(8,128)S(1)}, f32[8,128]{1,0:T(8,128)S(1)}, u32[]{:S(2)}, u32[]{:S(2)}) collective-permute-start(f32[8,128]{1,0:T(8,128)S(1)} %add.18), channel_id=1, source_target_pairs={{0,7},{1,6},{2,5},{3,4},{4,3},{5,2},{6,1},{7,0},{8,15},{9,14},{10,... | collective-permute-start | bytes 12296 | tf_op jit(solution)/shard_map/ppermute | solution.py:26
  79.0 1.6 %collective-permute-done.9 = f32[8,128]{1,0:T(8,128)S(1)} collective-permute-done((f32[8,128]{1,0:T(8,128)S(1)}, f32[8,128]{1,0:T(8,128)S(1)}, u32[]{:S(2)}, u32[]{:S(2)}) %collective-permute-start.9) | collective-permute-done | bytes 4128 | tf_op jit(solution)/shard_map/ppermute | solution.py:26
  80.5 4.2 %collective-permute-start.10 = (f32[8,128]{1,0:T(8,128)S(1)}, f32[8,128]{1,0:T(8,128)S(1)}, u32[]{:S(2)}, u32[]{:S(2)}) collective-permute-start(f32[8,128]{1,0:T(8,128)S(1)} %add.21), channel_id=1, source_target_pairs={{0,2},{1,3},{2,0},{3,1},{4,6},{5,7},{6,4},{7,5},{8,10},{9,11},{10,... | collective-permute-start | bytes 12296 | tf_op jit(solution)/shard_map/ppermute | solution.py:26
  84.7 1.9 %collective-permute-start.12 = (bf16[4,272,512]{2,1,0:T(8,128)(2,1)S(1)}, bf16[4,272,512]{2,1,0:T(8,128)(2,1)S(1)}, u32[]{:S(2)}, u32[]{:S(2)}) collective-permute-start(bf16[4,272,512]{2,1,0:T(8,128)(2,1)S(1)} %all-to-all-done.refs_0_), channel_id=1, source_target_pairs={{0,8},{8,0},{16,24},{24,16},{32,40},{40,32},{48,56},{56,48},{64,72... | collective-permute-start | bytes 3342344 | tf_op jit(solution)/shard_map/ppermute | solution.py:26
  86.6 0.3 collective-permute-done.10
  86.9 0.0 all-to-all-done.1.refs_2_
  86.9 2.1 %collective-permute-start.13 = (bf16[4,272,512]{2,1,0:T(8,128)(2,1)S(1)}, bf16[4,272,512]{2,1,0:T(8,128)(2,1)S(1)}, u32[]{:S(2)}, u32[]{:S(2)}) collective-permute-start(bf16[4,272,512]{2,1,0:T(8,128)(2,1)S(1)} %all-to-all-done.1.refs_2_), channel_id=1, source_target_pairs={{0,8},{8,0},{16,24},{24,16},{32,40},{40,32},{48,56},{56,48},{64,72... | collective-permute-start | bytes 3342344 | tf_op jit(solution)/shard_map/ppermute | solution.py:26
  89.1 5.5 %collective-permute-start.11 = (f32[8,128]{1,0:T(8,128)S(1)}, f32[8,128]{1,0:T(8,128)S(1)}, u32[]{:S(2)}, u32[]{:S(2)}) collective-permute-start(f32[8,128]{1,0:T(8,128)S(1)} %add.22), channel_id=1, source_target_pairs={{0,112},{8,120},{16,96},{24,104},{32,80},{40,88},{48,64},{56,72},{... | collective-permute-start | bytes 12296 | tf_op jit(solution)/shard_map/ppermute | solution.py:26
  94.6 3.0 %collective-permute-done.11 = f32[8,128]{1,0:T(8,128)S(1)} collective-permute-done((f32[8,128]{1,0:T(8,128)S(1)}, f32[8,128]{1,0:T(8,128)S(1)}, u32[]{:S(2)}, u32[]{:S(2)}) %collective-permute-start.11) | collective-permute-done | bytes 4128 | tf_op jit(solution)/shard_map/ppermute | solution.py:26
  97.6 0.0 collective-permute-done.12.refs_1_
  97.6 0.0 collective-permute-done.13.refs_3_
  97.6 2.3 %place.1 = bf16[1,4096,512]{2,1,0:T(8,128)(2,1)} custom-call(s32[1]{0:T(128)} %bitcast.position, f32[8,128]{1,0:T(8,128)S(1)} %add.23.sums, bf16[4,272,512]{2,1,0:T(8,128)(2,1)S(1)} %all-to-all-done.refs_0_, bf16[4,272,512]{2,1,0:T(8,128)(2,1)S(1)} %collective-permute-done.12.refs_1_, bf16[4,272,512]{2,1,0:T(8,128)(2,1)S(1)} %all-to-all-done.1.refs_2_, ...), custom_call_target="tpu_custom_call" | custom-call | tf_op jit(solution)/shard_map/place/pallas_call | solution.py:195
  (5 shorter events, 0.0 us)
Async XLA Ops:
  2.5 10.6 %collective-permute-start = (bf16[192,512]{1,0:T(8,128)(2,1)S(1)}, bf16[192,512]{1,0:T(8,128)(2,1)S(1)}, u32[]{:S(2)}, u32[]{:S(2)}) collective-permute-start(bf16[192,512]{1,0:T(8,128)(2,1)S(1)} %pad_maximum_fusion.refs_0_), channel_id=1, source_target_pairs={{0,32},{8,40},{16,48},{24,56},{32,0},{40,8},{48,16},{56,24},{64,96... | collective-permute-start | bytes 589832 | tf_op jit(solution)/shard_map/ppermute | solution.py:26
  4.7 19.2 %collective-permute-start.2 = (bf16[192,512]{1,0:T(8,128)(2,1)S(1)}, bf16[192,512]{1,0:T(8,128)(2,1)S(1)}, u32[]{:S(2)}, u32[]{:S(2)}) collective-permute-start(bf16[192,512]{1,0:T(8,128)(2,1)S(1)} %pad_maximum_fusion.refs_0_), channel_id=1, source_target_pairs={{0,16},{8,24},{16,0},{24,8},{32,48},{40,56},{48,32},{56,40},{64,80... | collective-permute-start | bytes 589832 | tf_op jit(solution)/shard_map/ppermute | solution.py:26
  13.1 12.8 %collective-permute-start.5 = (bf16[192,512]{1,0:T(8,128)(2,1)S(1)}, bf16[192,512]{1,0:T(8,128)(2,1)S(1)}, u32[]{:S(2)}, u32[]{:S(2)}) collective-permute-start(bf16[192,512]{1,0:T(8,128)(2,1)S(1)} %collective-permute-done.refs_4_), channel_id=1, source_target_pairs={{0,16},{8,24},{16,0},{24,8},{32,48},{40,56},{48,32},{56,40},{64,80... | collective-permute-start | bytes 589832 | tf_op jit(solution)/shard_map/ppermute | solution.py:26
  19.6 8.7 %collective-permute-start.1 = (bf16[192,512]{1,0:T(8,128)(2,1)S(1)}, bf16[192,512]{1,0:T(8,128)(2,1)S(1)}, u32[]{:S(2)}, u32[]{:S(2)}) collective-permute-start(bf16[192,512]{1,0:T(8,128)(2,1)S(1)} %pad_maximum_fusion.refs_0_), channel_id=1, source_target_pairs={{0,8},{8,0},{16,24},{24,16},{32,40},{40,32},{48,56},{56,48},{64,72... | collective-permute-start | bytes 589832 | tf_op jit(solution)/shard_map/ppermute | solution.py:26
  21.5 6.8 %collective-permute-start.4 = (bf16[192,512]{1,0:T(8,128)(2,1)S(1)}, bf16[192,512]{1,0:T(8,128)(2,1)S(1)}, u32[]{:S(2)}, u32[]{:S(2)}) collective-permute-start(bf16[192,512]{1,0:T(8,128)(2,1)S(1)} %collective-permute-done.refs_4_), channel_id=1, source_target_pairs={{0,8},{8,0},{16,24},{24,16},{32,40},{40,32},{48,56},{56,48},{64,72... | collective-permute-start | bytes 589832 | tf_op jit(solution)/shard_map/ppermute | solution.py:26
  24.0 4.4 %collective-permute-start.3 = (bf16[192,512]{1,0:T(8,128)(2,1)S(1)}, bf16[192,512]{1,0:T(8,128)(2,1)S(1)}, u32[]{:S(2)}, u32[]{:S(2)}) collective-permute-start(bf16[192,512]{1,0:T(8,128)(2,1)S(1)} %collective-permute-done.2.refs_2_), channel_id=1, source_target_pairs={{0,8},{8,0},{16,24},{24,16},{32,40},{40,32},{48,56},{56,48},{64,72... | collective-permute-start | bytes 589832 | tf_op jit(solution)/shard_map/ppermute | solution.py:26
  25.9 3.5 %collective-permute-start.6 = (bf16[192,512]{1,0:T(8,128)(2,1)S(1)}, bf16[192,512]{1,0:T(8,128)(2,1)S(1)}, u32[]{:S(2)}, u32[]{:S(2)}) collective-permute-start(bf16[192,512]{1,0:T(8,128)(2,1)S(1)} %collective-permute-done.5.refs_6_), channel_id=1, source_target_pairs={{0,8},{8,0},{16,24},{24,16},{32,40},{40,32},{48,56},{56,48},{64,72... | collective-permute-start | bytes 589832 | tf_op jit(solution)/shard_map/ppermute | solution.py:26
  39.3 21.0 %copy-start = (f32[1,64,512]{2,1,0:T(8,128)S(1)}, f32[1,64,512]{2,1,0:T(8,128)}, u32[]{:S(2)}) copy-start(f32[1,64,512]{2,1,0:T(8,128)} %param.6) | copy-start | bytes 393220
  39.3 21.0 %copy-start.1 = (f32[1,64,512]{2,1,0:T(8,128)S(1)}, f32[1,64,512]{2,1,0:T(8,128)}, u32[]{:S(2)}) copy-start(f32[1,64,512]{2,1,0:T(8,128)} %param.5) | copy-start | bytes 393220
  39.3 18.3 %all-to-all-start = ((bf16[4,272,512]{2,1,0:T(8,128)(2,1)}), bf16[4,272,512]{2,1,0:T(8,128)(2,1)S(1)}, u32[]{:S(2)}, u32[]{:S(2)}) async-start(bf16[4,272,512]{2,1,0:T(8,128)(2,1)} %get-tuple-element.17), calls=%async_computation | async-start | bytes 2228224 | tf_op jit(solution)/shard_map/all_to_all | solution.py:231
  42.9 20.2 %collective-permute-start.7 = (bf16[272,512]{1,0:T(8,128)(2,1)S(1)}, bf16[272,512]{1,0:T(8,128)(2,1)S(1)}, u32[]{:S(2)}, u32[]{:S(2)}) collective-permute-start(bf16[272,512]{1,0:T(8,128)(2,1)S(1)} %get-tuple-element.16), channel_id=1, source_target_pairs={{0,112},{8,120},{16,96},{24,104},{32,80},{40,88},{48,64},{56,72},{... | collective-permute-start | bytes 835592 | tf_op jit(solution)/shard_map/ppermute | solution.py:26
  57.6 5.5 %collective-permute-start.8 = (f32[8,128]{1,0:T(8,128)S(1)}, f32[8,128]{1,0:T(8,128)S(1)}, u32[]{:S(2)}, u32[]{:S(2)}) collective-permute-start(f32[8,128]{1,0:T(8,128)S(1)} %convert_reduce_fusion), channel_id=1, source_target_pairs={{0,1},{1,0},{2,3},{3,2},{4,5},{5,4},{6,7},{7,6},{8,9},{9,8},{10,11... | collective-permute-start | bytes 12296 | tf_op jit(solution)/shard_map/ppermute | solution.py:26
  64.2 22.8 %all-to-all-start.1 = ((bf16[4,272,512]{2,1,0:T(8,128)(2,1)}), bf16[4,272,512]{2,1,0:T(8,128)(2,1)S(1)}, u32[]{:S(2)}, u32[]{:S(2)}) async-start(bf16[4,272,512]{2,1,0:T(8,128)(2,1)} %spread.1), calls=%async_computation.1 | async-start | bytes 2228224 | tf_op jit(solution)/shard_map/all_to_all | solution.py:238
  69.1 11.4 %collective-permute-start.9 = (f32[8,128]{1,0:T(8,128)S(1)}, f32[8,128]{1,0:T(8,128)S(1)}, u32[]{:S(2)}, u32[]{:S(2)}) collective-permute-start(f32[8,128]{1,0:T(8,128)S(1)} %add.18), channel_id=1, source_target_pairs={{0,7},{1,6},{2,5},{3,4},{4,3},{5,2},{6,1},{7,0},{8,15},{9,14},{10,... | collective-permute-start | bytes 12296 | tf_op jit(solution)/shard_map/ppermute | solution.py:26
  80.5 6.4 %collective-permute-start.10 = (f32[8,128]{1,0:T(8,128)S(1)}, f32[8,128]{1,0:T(8,128)S(1)}, u32[]{:S(2)}, u32[]{:S(2)}) collective-permute-start(f32[8,128]{1,0:T(8,128)S(1)} %add.21), channel_id=1, source_target_pairs={{0,2},{1,3},{2,0},{3,1},{4,6},{5,7},{6,4},{7,5},{8,10},{9,11},{10,... | collective-permute-start | bytes 12296 | tf_op jit(solution)/shard_map/ppermute | solution.py:26
  84.7 12.9 %collective-permute-start.12 = (bf16[4,272,512]{2,1,0:T(8,128)(2,1)S(1)}, bf16[4,272,512]{2,1,0:T(8,128)(2,1)S(1)}, u32[]{:S(2)}, u32[]{:S(2)}) collective-permute-start(bf16[4,272,512]{2,1,0:T(8,128)(2,1)S(1)} %all-to-all-done.refs_0_), channel_id=1, source_target_pairs={{0,8},{8,0},{16,24},{24,16},{32,40},{40,32},{48,56},{56,48},{64,72... | collective-permute-start | bytes 3342344 | tf_op jit(solution)/shard_map/ppermute | solution.py:26
  86.9 10.7 %collective-permute-start.13 = (bf16[4,272,512]{2,1,0:T(8,128)(2,1)S(1)}, bf16[4,272,512]{2,1,0:T(8,128)(2,1)S(1)}, u32[]{:S(2)}, u32[]{:S(2)}) collective-permute-start(bf16[4,272,512]{2,1,0:T(8,128)(2,1)S(1)} %all-to-all-done.1.refs_2_), channel_id=1, source_target_pairs={{0,8},{8,0},{16,24},{24,16},{32,40},{40,32},{48,56},{56,48},{64,72... | collective-permute-start | bytes 3342344 | tf_op jit(solution)/shard_map/ppermute | solution.py:26
  89.1 8.5 %collective-permute-start.11 = (f32[8,128]{1,0:T(8,128)S(1)}, f32[8,128]{1,0:T(8,128)S(1)}, u32[]{:S(2)}, u32[]{:S(2)}) collective-permute-start(f32[8,128]{1,0:T(8,128)S(1)} %add.22), channel_id=1, source_target_pairs={{0,112},{8,120},{16,96},{24,104},{32,80},{40,88},{48,64},{56,72},{... | collective-permute-start | bytes 12296 | tf_op jit(solution)/shard_map/ppermute | solution.py:26

commit v3 on v2

--- a/solution.py
+++ b/solution.py
@@ -9,7 +9,6 @@
 SLAB = 64
 ORDER = 512
 HALF = ORDER // 2
-SENT = HALF + 16
 PANEL = 256
 COLUMNS = 4
 
@@ -34,17 +33,9 @@
     return value.astype(jnp.bfloat16)
 
 
-def thirds(value):
-    parts = []
-    for _ in range(3):
-        parts.append(jnp.broadcast_to(short(value), (1, ORDER)))
-        value = value - short(value).astype(jnp.float32)
-    return parts
-
-
 def refresh_kernel(position, steps, *refs):
     pieces = refs[:8]
-    products_out, half_out, copies_out = refs[8:11]
+    products_out, half_out, sums_out = refs[8:11]
     grad, old_left, old_right, low, low_square, fourth, short_total, work, poly, total = refs[11:]
     member = position[0] & (GROUP - 1)
     block = position[0] // GROUP
@@ -131,12 +122,9 @@
         total[rows, :] = value
         cond_square = cond_square + jnp.sum(value * value, keepdims=True)
     half = short(total[pl.ds(pl.multiple_of((member & 1) * HALF, HALF), HALF), :])
-    half_out[0:HALF, :] = half
-    half_out[HALF:, :] = jnp.concatenate(
-        thirds(cond_square) + thirds(grad_square) + [jnp.zeros((10, ORDER), jnp.bfloat16)], axis=0
-    )
-    for column in range(COLUMNS):
-        copies_out[column] = half_out[...]
+    half_out[...] = half
+    row = lax.broadcasted_iota(jnp.int32, (8, 128), 0)
+    sums_out[...] = jnp.where(row < 4, cond_square, grad_square)
 
 
 def refresh(position, steps, pieces):
@@ -145,8 +133,8 @@
         refresh_kernel,
         out_shape=(
             jax.ShapeDtypeStruct((2, SLAB, ORDER), jnp.float32),
-            jax.ShapeDtypeStruct((SENT, ORDER), jnp.bfloat16),
-            jax.ShapeDtypeStruct((COLUMNS, SENT, ORDER), jnp.bfloat16),
+            jax.ShapeDtypeStruct((HALF, ORDER), jnp.bfloat16),
+            jax.ShapeDtypeStruct((8, 128), jnp.float32),
         ),
         in_specs=[SMEM] * 2 + [VMEM] * 8,
         out_specs=(VMEM,) * 3,
@@ -156,32 +144,34 @@
     )(position, steps, *pieces)
 
 
-def spread_kernel(half, out):
+def spread_kernel(half, mirrored, out):
     for column in range(COLUMNS):
-        out[column] = half[...]
-
-
-def spread(half):
+        out[column, 0:HALF, :] = half[...]
+        out[column, HALF:, :] = mirrored[...]
+
+
+def spread(half, mirrored):
     return pl.pallas_call(
         spread_kernel,
-        out_shape=jax.ShapeDtypeStruct((COLUMNS, *half.shape), half.dtype),
-        in_specs=[VMEM],
+        out_shape=jax.ShapeDtypeStruct((COLUMNS, ORDER, ORDER), jnp.bfloat16),
+        in_specs=[VMEM] * 2,
         out_specs=VMEM,
         compiler_params=PARAMS,
         name="spread",
-    )(half)
+    )(half, mirrored)
 
 
 def place_kernel(position, sums, *refs):
-    sources, out, staged, sems = refs[:4], refs[4], refs[5], refs[6]
-    squares = [sums[i : i + 1] + sums[i + 1 : i + 2] + sums[i + 2 : i + 3] for i in (0, 3)]
-    ratio = jnp.sqrt(squares[1] / (squares[0] + epsilon))[:, 0:1]
+    sources, out, staged, sems = refs[:2], refs[2], refs[3], refs[4]
+    ratio = jnp.sqrt(sums[4:5, 0:1] / (sums[0:1, 0:1] + epsilon))
     slot = ((position[0] // GROUP) & 1) * 2 + (position[0] & 1)
     stores = []
-    for relative, source in enumerate(sources):
+    for relative in range(4):
+        first = relative // 2 * HALF
         for column in range(COLUMNS):
             index = relative * COLUMNS + column
-            staged[index] = short(source[column, 0:HALF].astype(jnp.float32) * ratio)
+            piece = sources[relative & 1][column, first : first + HALF]
+            staged[index] = short(piece.astype(jnp.float32) * ratio)
             row = (column * 4 + (slot ^ relative)) * HALF
             rows = pl.ds(pl.multiple_of(row, HALF), HALF)
             store = pltpu.make_async_copy(staged.at[index], out.at[0, rows], sems.at[index])
@@ -195,7 +185,7 @@
     return pl.pallas_call(
         place_kernel,
         out_shape=jax.ShapeDtypeStruct((1, 4 * COLUMNS * HALF, ORDER), jnp.bfloat16),
-        in_specs=[SMEM] + [VMEM] * 5,
+        in_specs=[SMEM] + [VMEM] * 3,
         out_specs=HBM,
         scratch_shapes=[
             pltpu.VMEM((4 * COLUMNS, HALF, ORDER), jnp.bfloat16),
@@ -206,14 +196,12 @@
     )(position, sums, *sources)
 
 
-def tally(blocks):
-    return jnp.sum(blocks[:, HALF : HALF + 8, 0:128].astype(jnp.float32), axis=0)
-
-
 def per_device(grads, left_old, right_old, root_steps):
     position = jnp.reshape(lax.axis_index("dp"), (1,))
     steps = jnp.reshape(root_steps, (16,))
-    own = short(jnp.concatenate([grads[0].astype(jnp.float32), left_old[0], right_old[0]], axis=0))
+    part = lax.broadcasted_iota(jnp.int32, (3, 1, 1), 0)
+    olds = jnp.where(part == 1, left_old, right_old)
+    own = jnp.where(part == 0, grads, short(olds)).reshape(3 * SLAB, ORDER)
     far = flipped(own, "dp", 4)
     near = flipped(own, "dp", 2)
     far, steps = lax.optimization_barrier((far, steps))
@@ -222,27 +210,26 @@
     for relative, piece in ((0, own), (2, near), (4, far), (6, both)):
         pieces[relative] = piece
         pieces[relative + 1] = flipped(piece, "dp", 1)
-    products, half, copies = refresh(position, steps, pieces)
+    products, half, sums = refresh(position, steps, pieces)
     left_rows = decay_rate * left_old + products[0:1]
     right_rows = decay_rate * right_old + products[1:2]
 
     columns = [[16 * i + k for i in range(COLUMNS)] for k in range(16)]
     mirrored = flipped(half, "dp", 14)
-    same = lax.all_to_all(copies, "dp", 0, 0, axis_index_groups=columns)
-    sums = tally(same)
-    sums = sums + flipped(sums, "shard", 1)
+    for mask in (1, 2):
+        sums = sums + flipped(sums, "shard", mask)
     mirrored, sums, left_rows, right_rows = lax.optimization_barrier(
         (mirrored, sums, left_rows, right_rows)
     )
-    mirrored = spread(mirrored)
-    cross = lax.all_to_all(mirrored, "dp", 0, 0, axis_index_groups=columns)
-    same_other = flipped(same, "dp", 1)
-    for mask in (7, 2):
-        sums = sums + flipped(sums, "shard", mask)
-    cross, sums = lax.optimization_barrier((cross, sums))
-    cross_other = flipped(cross, "dp", 1)
-    sums = sums + flipped(sums, "dp", 14)
-    update = place(position, sums, [same, same_other, cross, cross_other])
+    copies = spread(half, mirrored)
+    mine = lax.all_to_all(copies, "dp", 0, 0, axis_index_groups=columns)
+    sums = sums + flipped(sums, "shard", 7)
+    for mask in (14, 16):
+        sums = sums + flipped(sums, "dp", mask)
+    mine, sums = lax.optimization_barrier((mine, sums))
+    other = flipped(mine, "dp", 1)
+    sums = sums + flipped(sums, "dp", 32)
+    update = place(position, sums, [mine, other])
     return (update, left_rows, right_rows)
 
 

time: 101 us -> 100 us (0.990)
  starting transfers between devices: 59.7 us -> 67.4 us
  Pallas kernels: 13.2 us -> 7.22 us
  waiting for transfers between devices: 22.7 us -> 21 us
    ppermute x14 -> x15, starting transfers between devices: 51.1 us -> 62.2 us  [flipped(): lax.ppermute(value, axis, [(i, i ^ mask) for i in range(lax.axis_size(axi...]
    all_to_all x2 -> x1, waiting for transfers between devices: 10.7 us -> 0.01 us  [per_device(): mine = lax.all_to_all(copies, 'dp', 0, 0, axis_index_groups=columns)]
    ppermute x14 -> x15, waiting for transfers between devices: 12 us -> 21 us  [flipped(): lax.ppermute(value, axis, [(i, i ^ mask) for i in range(lax.axis_size(axi...]
    pallas_call x1, Pallas kernels: 9.92 us -> 3.52 us  [refresh(): pl.pallas_call(refresh_kernel, out_shape=(jax.ShapeDtypeStruct((2, SLAB,...]
    all_to_all x2 -> x1, starting transfers between devices: 8.6 us -> 5.22 us  [per_device(): mine = lax.all_to_all(copies, 'dp', 0, 0, axis_index_groups=columns)]
    select_n x0 -> x1, other arithmetic: none -> 1.09 us  [per_device(): own = jnp.where(part == 0, grads, short(olds)).reshape(3 * SLAB, ORDER)]
  transfers between devices with their start and end apart: 16 -> 16, of which waited for: 7 -> 8; matrix products, arithmetic and copies ran while one was open for 2% -> 2% of each run, Pallas kernels for 0% -> 0%
where the time goes in v3:
time: 100 us; the launch traced here: 99.5 us
  starting transfers between devices  67.4 us (67%)
  waiting for transfers between devices  21 us (21%)
  Pallas kernels  7.22 us (7%)
  other arithmetic  1.86 us (2%)
  local copies, waits for them, and re-layouts  1.17 us (1%)
    ppermute x15, starting transfers between devices, flipped(): lax.ppermute(value, axis, [(i, i ^ mask) for i in range(lax.axis_size(axi...  62.2 us
    ppermute x15, waiting for transfers between devices, flipped(): lax.ppermute(value, axis, [(i, i ^ mask) for i in range(lax.axis_size(axi...  21 us
    all_to_all x1, starting transfers between devices, per_device(): mine = lax.all_to_all(copies, 'dp', 0, 0, axis_index_groups=columns)  5.22 us
    pallas_call x1, Pallas kernels, refresh(): pl.pallas_call(refresh_kernel, out_shape=(jax.ShapeDtypeStruct((2, SLAB,...  3.52 us
    pallas_call x1, Pallas kernels, place(): pl.pallas_call(place_kernel, out_shape=jax.ShapeDtypeStruct((1, 4 * COLUM...  2.24 us
  transfers between devices with their start and end apart: 16, of which 8 were waited for; matrix products, arithmetic and copies ran while one was open for 2% of the time, Pallas kernels for 0%

profile of v3, /device:TPU:18, one launch (start us, length us, event | category | flops | bytes accessed | tf_op | source)
XLA Modules:
  0.0 99.5 jit_solution(2483821272557344158)
XLA Ops:
  0.6 0.0 copy-start.1
  0.6 0.0 copy-start
  0.7 0.1 broadcast_in_dim.60
  0.8 0.1 broadcast_in_dim.61
  0.8 0.1 broadcast_in_dim.66
  0.9 0.1 broadcast_in_dim.67
  1.0 1.1 %fusion.1.refs_0_ = bf16[192,512]{1,0:T(8,128)(2,1)S(1)} fusion(f32[64,512]{1,0:T(8,128)} %bitcast.16, f32[64,512]{1,0:T(8,128)} %bitcast.17, pred[192]{0:T(512)(128)(4,1)S(1)} %broadcast_in_dim.67, pred[192]{0:T(512)(128)(4,1)S(1)} %broadcast_in_dim.61, bf16[64,512]{1,0:T(8,128)(2,1)} %bitcast.18), kind=kLoop, calls=%fused_computation.2 | loop fusion | flops 196608 | bytes 524672 | tf_op jit(solution)/shard_map/jit(_where)/select_n | solution.py:204
  2.1 2.2 %collective-permute-start = (bf16[192,512]{1,0:T(8,128)(2,1)S(1)}, bf16[192,512]{1,0:T(8,128)(2,1)S(1)}, u32[]{:S(2)}, u32[]{:S(2)}) collective-permute-start(bf16[192,512]{1,0:T(8,128)(2,1)S(1)} %fusion.1.refs_0_), channel_id=1, source_target_pairs={{0,32},{8,40},{16,48},{24,56},{32,0},{40,8},{48,16},{56,24},{64,96... | collective-permute-start | bytes 589832 | tf_op jit(solution)/shard_map/ppermute | solution.py:25
  4.3 3.5 %collective-permute-start.2 = (bf16[192,512]{1,0:T(8,128)(2,1)S(1)}, bf16[192,512]{1,0:T(8,128)(2,1)S(1)}, u32[]{:S(2)}, u32[]{:S(2)}) collective-permute-start(bf16[192,512]{1,0:T(8,128)(2,1)S(1)} %fusion.1.refs_0_), channel_id=1, source_target_pairs={{0,16},{8,24},{16,0},{24,8},{32,48},{40,56},{48,32},{56,40},{64,80... | collective-permute-start | bytes 589832 | tf_op jit(solution)/shard_map/ppermute | solution.py:25
  7.8 0.8 copy.8
  8.6 0.1 reshape.29.steps
  8.7 4.1 %collective-permute-done.refs_4_ = bf16[192,512]{1,0:T(8,128)(2,1)S(1)} collective-permute-done((bf16[192,512]{1,0:T(8,128)(2,1)S(1)}, bf16[192,512]{1,0:T(8,128)(2,1)S(1)}, u32[]{:S(2)}, u32[]{:S(2)}) %collective-permute-start) | collective-permute-done | bytes 196640 | tf_op jit(solution)/shard_map/ppermute | solution.py:25
  12.7 6.5 %collective-permute-start.5 = (bf16[192,512]{1,0:T(8,128)(2,1)S(1)}, bf16[192,512]{1,0:T(8,128)(2,1)S(1)}, u32[]{:S(2)}, u32[]{:S(2)}) collective-permute-start(bf16[192,512]{1,0:T(8,128)(2,1)S(1)} %collective-permute-done.refs_4_), channel_id=1, source_target_pairs={{0,16},{8,24},{16,0},{24,8},{32,48},{40,56},{48,32},{56,40},{64,80... | collective-permute-start | bytes 589832 | tf_op jit(solution)/shard_map/ppermute | solution.py:25
  19.2 1.9 %collective-permute-start.1 = (bf16[192,512]{1,0:T(8,128)(2,1)S(1)}, bf16[192,512]{1,0:T(8,128)(2,1)S(1)}, u32[]{:S(2)}, u32[]{:S(2)}) collective-permute-start(bf16[192,512]{1,0:T(8,128)(2,1)S(1)} %fusion.1.refs_0_), channel_id=1, source_target_pairs={{0,8},{8,0},{16,24},{24,16},{32,40},{40,32},{48,56},{56,48},{64,72... | collective-permute-start | bytes 589832 | tf_op jit(solution)/shard_map/ppermute | solution.py:25
  21.1 2.4 %collective-permute-start.4 = (bf16[192,512]{1,0:T(8,128)(2,1)S(1)}, bf16[192,512]{1,0:T(8,128)(2,1)S(1)}, u32[]{:S(2)}, u32[]{:S(2)}) collective-permute-start(bf16[192,512]{1,0:T(8,128)(2,1)S(1)} %collective-permute-done.refs_4_), channel_id=1, source_target_pairs={{0,8},{8,0},{16,24},{24,16},{32,40},{40,32},{48,56},{56,48},{64,72... | collective-permute-start | bytes 589832 | tf_op jit(solution)/shard_map/ppermute | solution.py:25
  23.6 0.0 collective-permute-done.2.refs_2_
  23.6 1.9 %collective-permute-start.3 = (bf16[192,512]{1,0:T(8,128)(2,1)S(1)}, bf16[192,512]{1,0:T(8,128)(2,1)S(1)}, u32[]{:S(2)}, u32[]{:S(2)}) collective-permute-start(bf16[192,512]{1,0:T(8,128)(2,1)S(1)} %collective-permute-done.2.refs_2_), channel_id=1, source_target_pairs={{0,8},{8,0},{16,24},{24,16},{32,40},{40,32},{48,56},{56,48},{64,72... | collective-permute-start | bytes 589832 | tf_op jit(solution)/shard_map/ppermute | solution.py:25
  25.5 0.0 collective-permute-done.5.refs_6_
  25.5 2.4 %collective-permute-start.6 = (bf16[192,512]{1,0:T(8,128)(2,1)S(1)}, bf16[192,512]{1,0:T(8,128)(2,1)S(1)}, u32[]{:S(2)}, u32[]{:S(2)}) collective-permute-start(bf16[192,512]{1,0:T(8,128)(2,1)S(1)} %collective-permute-done.5.refs_6_), channel_id=1, source_target_pairs={{0,8},{8,0},{16,24},{24,16},{32,40},{40,32},{48,56},{56,48},{64,72... | collective-permute-start | bytes 589832 | tf_op jit(solution)/shard_map/ppermute | solution.py:25
  27.9 0.0 collective-permute-done.1.refs_1_
  27.9 0.0 collective-permute-done.3.refs_3_
  27.9 0.0 collective-permute-done.4.refs_5_
  28.0 1.0 %collective-permute-done.6.refs_7_ = bf16[192,512]{1,0:T(8,128)(2,1)S(1)} collective-permute-done((bf16[192,512]{1,0:T(8,128)(2,1)S(1)}, bf16[192,512]{1,0:T(8,128)(2,1)S(1)}, u32[]{:S(2)}, u32[]{:S(2)}) %collective-permute-start.6) | collective-permute-done | bytes 196640 | tf_op jit(solution)/shard_map/ppermute | solution.py:25
  29.0 3.5 %refresh.1 = (f32[2,64,512]{2,1,0:T(8,128)S(1)}, bf16[256,512]{1,0:T(8,128)(2,1)S(1)}, f32[8,128]{1,0:T(8,128)S(1)}) custom-call(s32[1]{0:T(128)} %bitcast.position, s32[16]{0:T(128)S(1)} %reshape.29.steps, bf16[192,512]{1,0:T(8,128)(2,1)S(1)} %fusion.1.refs_0_, bf16[192,512]{1,0:T(8,128)(2,1)S(1)} %collective-permute-done.1.refs_1_, ...), custom_call_target="tpu_custom_call" | custom-call | tf_op jit(solution)/shard_map/refresh/pallas_call | solution.py:132
  32.5 5.7 %collective-permute-start.7 = (bf16[256,512]{1,0:T(8,128)(2,1)S(1)}, bf16[256,512]{1,0:T(8,128)(2,1)S(1)}, u32[]{:S(2)}, u32[]{:S(2)}) collective-permute-start(bf16[256,512]{1,0:T(8,128)(2,1)S(1)} %get-tuple-element.16.half), channel_id=1, source_target_pairs={{0,112},{8,120},{16,96},{24,104},{32,80},{40,88},{48,64},{56,72},{... | collective-permute-start | bytes 786440 | tf_op jit(solution)/shard_map/ppermute | solution.py:25
  38.2 5.6 %collective-permute-start.8 = (f32[8,128]{1,0:T(8,128)S(1)}, f32[8,128]{1,0:T(8,128)S(1)}, u32[]{:S(2)}, u32[]{:S(2)}) collective-permute-start(f32[8,128]{1,0:T(8,128)S(1)} %get-tuple-element.17), channel_id=1, source_target_pairs={{0,1},{1,0},{2,3},{3,2},{4,5},{5,4},{6,7},{7,6},{8,9},{9,8},{10,11... | collective-permute-start | bytes 12296 | tf_op jit(solution)/shard_map/ppermute | solution.py:25
  43.8 1.6 %collective-permute-done.8 = f32[8,128]{1,0:T(8,128)S(1)} collective-permute-done((f32[8,128]{1,0:T(8,128)S(1)}, f32[8,128]{1,0:T(8,128)S(1)}, u32[]{:S(2)}, u32[]{:S(2)}) %collective-permute-start.8) | collective-permute-done | bytes 4128 | tf_op jit(solution)/shard_map/ppermute | solution.py:25
  45.4 9.8 %collective-permute-start.9 = (f32[8,128]{1,0:T(8,128)S(1)}, f32[8,128]{1,0:T(8,128)S(1)}, u32[]{:S(2)}, u32[]{:S(2)}) collective-permute-start(f32[8,128]{1,0:T(8,128)S(1)} %add.24), channel_id=1, source_target_pairs={{0,2},{1,3},{2,0},{3,1},{4,6},{5,7},{6,4},{7,5},{8,10},{9,11},{10,... | collective-permute-start | bytes 12296 | tf_op jit(solution)/shard_map/ppermute | solution.py:25
  55.2 0.0 copy-done.1
  55.2 0.0 copy-done
  55.2 0.7 slice_add_fusion
  56.0 0.8 collective-permute-done.9
  56.8 0.0 collective-permute-done.7.mirrored
  56.8 1.5 %spread.1 = bf16[4,512,512]{2,1,0:T(8,128)(2,1)} custom-call(bf16[256,512]{1,0:T(8,128)(2,1)S(1)} %get-tuple-element.16.half, bf16[256,512]{1,0:T(8,128)(2,1)S(1)} %collective-permute-done.7.mirrored), custom_call_target="tpu_custom_call" | custom-call | tf_op jit(solution)/shard_map/spread/pallas_call | solution.py:154
  58.3 5.2 %all-to-all-start = ((bf16[4,512,512]{2,1,0:T(8,128)(2,1)}), bf16[4,512,512]{2,1,0:T(8,128)(2,1)S(1)}, u32[]{:S(2)}, u32[]{:S(2)}) async-start(bf16[4,512,512]{2,1,0:T(8,128)(2,1)} %spread.1), calls=%async_computation | async-start | bytes 4194304 | tf_op jit(solution)/shard_map/all_to_all | solution.py:225
  63.5 9.3 %collective-permute-start.10 = (f32[8,128]{1,0:T(8,128)S(1)}, f32[8,128]{1,0:T(8,128)S(1)}, u32[]{:S(2)}, u32[]{:S(2)}) collective-permute-start(f32[8,128]{1,0:T(8,128)S(1)} %add.25), channel_id=1, source_target_pairs={{0,7},{1,6},{2,5},{3,4},{4,3},{5,2},{6,1},{7,0},{8,15},{9,14},{10,... | collective-permute-start | bytes 12296 | tf_op jit(solution)/shard_map/ppermute | solution.py:25
  72.8 1.6 %collective-permute-done.10 = f32[8,128]{1,0:T(8,128)S(1)} collective-permute-done((f32[8,128]{1,0:T(8,128)S(1)}, f32[8,128]{1,0:T(8,128)S(1)}, u32[]{:S(2)}, u32[]{:S(2)}) %collective-permute-start.10) | collective-permute-done | bytes 4128 | tf_op jit(solution)/shard_map/ppermute | solution.py:25
  74.3 3.1 %collective-permute-start.11 = (f32[8,128]{1,0:T(8,128)S(1)}, f32[8,128]{1,0:T(8,128)S(1)}, u32[]{:S(2)}, u32[]{:S(2)}) collective-permute-start(f32[8,128]{1,0:T(8,128)S(1)} %add.28), channel_id=1, source_target_pairs={{0,112},{8,120},{16,96},{24,104},{32,80},{40,88},{48,64},{56,72},{... | collective-permute-start | bytes 12296 | tf_op jit(solution)/shard_map/ppermute | solution.py:25
  77.5 5.4 %collective-permute-done.11 = f32[8,128]{1,0:T(8,128)S(1)} collective-permute-done((f32[8,128]{1,0:T(8,128)S(1)}, f32[8,128]{1,0:T(8,128)S(1)}, u32[]{:S(2)}, u32[]{:S(2)}) %collective-permute-start.11) | collective-permute-done | bytes 4128 | tf_op jit(solution)/shard_map/ppermute | solution.py:25
  82.8 1.9 %collective-permute-start.12 = (f32[8,128]{1,0:T(8,128)S(1)}, f32[8,128]{1,0:T(8,128)S(1)}, u32[]{:S(2)}, u32[]{:S(2)}) collective-permute-start(f32[8,128]{1,0:T(8,128)S(1)} %add.29), channel_id=1, source_target_pairs={{0,128},{8,136},{16,144},{24,152},{32,160},{40,168},{48,176},{56,1... | collective-permute-start | bytes 12296 | tf_op jit(solution)/shard_map/ppermute | solution.py:25
  84.7 3.6 %collective-permute-done.12 = f32[8,128]{1,0:T(8,128)S(1)} collective-permute-done((f32[8,128]{1,0:T(8,128)S(1)}, f32[8,128]{1,0:T(8,128)S(1)}, u32[]{:S(2)}, u32[]{:S(2)}) %collective-permute-start.12) | collective-permute-done | bytes 4128 | tf_op jit(solution)/shard_map/ppermute | solution.py:25
  88.3 0.0 all-to-all-done.refs_0_
  88.3 1.9 %collective-permute-start.14 = (bf16[4,512,512]{2,1,0:T(8,128)(2,1)S(1)}, bf16[4,512,512]{2,1,0:T(8,128)(2,1)S(1)}, u32[]{:S(2)}, u32[]{:S(2)}) collective-permute-start(bf16[4,512,512]{2,1,0:T(8,128)(2,1)S(1)} %all-to-all-done.refs_0_), channel_id=1, source_target_pairs={{0,8},{8,0},{16,24},{24,16},{32,40},{40,32},{48,56},{56,48},{64,72... | collective-permute-start | bytes 6291464 | tf_op jit(solution)/shard_map/ppermute | solution.py:25
  90.2 4.0 %collective-permute-start.13 = (f32[8,128]{1,0:T(8,128)S(1)}, f32[8,128]{1,0:T(8,128)S(1)}, u32[]{:S(2)}, u32[]{:S(2)}) collective-permute-start(f32[8,128]{1,0:T(8,128)S(1)} %add.30), channel_id=1, source_target_pairs={{0,256},{8,264},{16,272},{24,280},{32,288},{40,296},{48,304},{56,3... | collective-permute-start | bytes 12296 | tf_op jit(solution)/shard_map/ppermute | solution.py:25
  94.2 3.0 %collective-permute-done.13 = f32[8,128]{1,0:T(8,128)S(1)} collective-permute-done((f32[8,128]{1,0:T(8,128)S(1)}, f32[8,128]{1,0:T(8,128)S(1)}, u32[]{:S(2)}, u32[]{:S(2)}) %collective-permute-start.13) | collective-permute-done | bytes 4128 | tf_op jit(solution)/shard_map/ppermute | solution.py:25
  97.3 0.0 collective-permute-done.14.refs_1_
  97.3 2.2 %place.1 = bf16[1,4096,512]{2,1,0:T(8,128)(2,1)} custom-call(s32[1]{0:T(128)} %bitcast.position, f32[8,128]{1,0:T(8,128)S(1)} %add.31.sums, bf16[4,512,512]{2,1,0:T(8,128)(2,1)S(1)} %all-to-all-done.refs_0_, bf16[4,512,512]{2,1,0:T(8,128)(2,1)S(1)} %collective-permute-done.14.refs_1_), custom_call_target="tpu_custom_call" | custom-call | tf_op jit(solution)/shard_map/place/pallas_call | solution.py:185
  (8 shorter events, 0.0 us)
Async XLA Ops:
  0.6 54.6 %copy-start.1 = (f32[1,64,512]{2,1,0:T(8,128)S(1)}, f32[1,64,512]{2,1,0:T(8,128)}, u32[]{:S(2)}) copy-start(f32[1,64,512]{2,1,0:T(8,128)} %param.5) | copy-start | bytes 393220
  0.6 54.6 %copy-start = (f32[1,64,512]{2,1,0:T(8,128)S(1)}, f32[1,64,512]{2,1,0:T(8,128)}, u32[]{:S(2)}) copy-start(f32[1,64,512]{2,1,0:T(8,128)} %param.6) | copy-start | bytes 393220
  2.1 10.6 %collective-permute-start = (bf16[192,512]{1,0:T(8,128)(2,1)S(1)}, bf16[192,512]{1,0:T(8,128)(2,1)S(1)}, u32[]{:S(2)}, u32[]{:S(2)}) collective-permute-start(bf16[192,512]{1,0:T(8,128)(2,1)S(1)} %fusion.1.refs_0_), channel_id=1, source_target_pairs={{0,32},{8,40},{16,48},{24,56},{32,0},{40,8},{48,16},{56,24},{64,96... | collective-permute-start | bytes 589832 | tf_op jit(solution)/shard_map/ppermute | solution.py:25
  4.3 19.2 %collective-permute-start.2 = (bf16[192,512]{1,0:T(8,128)(2,1)S(1)}, bf16[192,512]{1,0:T(8,128)(2,1)S(1)}, u32[]{:S(2)}, u32[]{:S(2)}) collective-permute-start(bf16[192,512]{1,0:T(8,128)(2,1)S(1)} %fusion.1.refs_0_), channel_id=1, source_target_pairs={{0,16},{8,24},{16,0},{24,8},{32,48},{40,56},{48,32},{56,40},{64,80... | collective-permute-start | bytes 589832 | tf_op jit(solution)/shard_map/ppermute | solution.py:25
  12.7 12.8 %collective-permute-start.5 = (bf16[192,512]{1,0:T(8,128)(2,1)S(1)}, bf16[192,512]{1,0:T(8,128)(2,1)S(1)}, u32[]{:S(2)}, u32[]{:S(2)}) collective-permute-start(bf16[192,512]{1,0:T(8,128)(2,1)S(1)} %collective-permute-done.refs_4_), channel_id=1, source_target_pairs={{0,16},{8,24},{16,0},{24,8},{32,48},{40,56},{48,32},{56,40},{64,80... | collective-permute-start | bytes 589832 | tf_op jit(solution)/shard_map/ppermute | solution.py:25
  19.2 8.7 %collective-permute-start.1 = (bf16[192,512]{1,0:T(8,128)(2,1)S(1)}, bf16[192,512]{1,0:T(8,128)(2,1)S(1)}, u32[]{:S(2)}, u32[]{:S(2)}) collective-permute-start(bf16[192,512]{1,0:T(8,128)(2,1)S(1)} %fusion.1.refs_0_), channel_id=1, source_target_pairs={{0,8},{8,0},{16,24},{24,16},{32,40},{40,32},{48,56},{56,48},{64,72... | collective-permute-start | bytes 589832 | tf_op jit(solution)/shard_map/ppermute | solution.py:25
  21.1 6.8 %collective-permute-start.4 = (bf16[192,512]{1,0:T(8,128)(2,1)S(1)}, bf16[192,512]{1,0:T(8,128)(2,1)S(1)}, u32[]{:S(2)}, u32[]{:S(2)}) collective-permute-start(bf16[192,512]{1,0:T(8,128)(2,1)S(1)} %collective-permute-done.refs_4_), channel_id=1, source_target_pairs={{0,8},{8,0},{16,24},{24,16},{32,40},{40,32},{48,56},{56,48},{64,72... | collective-permute-start | bytes 589832 | tf_op jit(solution)/shard_map/ppermute | solution.py:25
  23.6 4.4 %collective-permute-start.3 = (bf16[192,512]{1,0:T(8,128)(2,1)S(1)}, bf16[192,512]{1,0:T(8,128)(2,1)S(1)}, u32[]{:S(2)}, u32[]{:S(2)}) collective-permute-start(bf16[192,512]{1,0:T(8,128)(2,1)S(1)} %collective-permute-done.2.refs_2_), channel_id=1, source_target_pairs={{0,8},{8,0},{16,24},{24,16},{32,40},{40,32},{48,56},{56,48},{64,72... | collective-permute-start | bytes 589832 | tf_op jit(solution)/shard_map/ppermute | solution.py:25
  25.5 3.5 %collective-permute-start.6 = (bf16[192,512]{1,0:T(8,128)(2,1)S(1)}, bf16[192,512]{1,0:T(8,128)(2,1)S(1)}, u32[]{:S(2)}, u32[]{:S(2)}) collective-permute-start(bf16[192,512]{1,0:T(8,128)(2,1)S(1)} %collective-permute-done.5.refs_6_), channel_id=1, source_target_pairs={{0,8},{8,0},{16,24},{24,16},{32,40},{40,32},{48,56},{56,48},{64,72... | collective-permute-start | bytes 589832 | tf_op jit(solution)/shard_map/ppermute | solution.py:25
  32.5 24.3 %collective-permute-start.7 = (bf16[256,512]{1,0:T(8,128)(2,1)S(1)}, bf16[256,512]{1,0:T(8,128)(2,1)S(1)}, u32[]{:S(2)}, u32[]{:S(2)}) collective-permute-start(bf16[256,512]{1,0:T(8,128)(2,1)S(1)} %get-tuple-element.16.half), channel_id=1, source_target_pairs={{0,112},{8,120},{16,96},{24,104},{32,80},{40,88},{48,64},{56,72},{... | collective-permute-start | bytes 786440 | tf_op jit(solution)/shard_map/ppermute | solution.py:25
  38.2 7.2 %collective-permute-start.8 = (f32[8,128]{1,0:T(8,128)S(1)}, f32[8,128]{1,0:T(8,128)S(1)}, u32[]{:S(2)}, u32[]{:S(2)}) collective-permute-start(f32[8,128]{1,0:T(8,128)S(1)} %get-tuple-element.17), channel_id=1, source_target_pairs={{0,1},{1,0},{2,3},{3,2},{4,5},{5,4},{6,7},{7,6},{8,9},{9,8},{10,11... | collective-permute-start | bytes 12296 | tf_op jit(solution)/shard_map/ppermute | solution.py:25
  45.4 11.4 %collective-permute-start.9 = (f32[8,128]{1,0:T(8,128)S(1)}, f32[8,128]{1,0:T(8,128)S(1)}, u32[]{:S(2)}, u32[]{:S(2)}) collective-permute-start(f32[8,128]{1,0:T(8,128)S(1)} %add.24), channel_id=1, source_target_pairs={{0,2},{1,3},{2,0},{3,1},{4,6},{5,7},{6,4},{7,5},{8,10},{9,11},{10,... | collective-permute-start | bytes 12296 | tf_op jit(solution)/shard_map/ppermute | solution.py:25
  58.3 30.1 %all-to-all-start = ((bf16[4,512,512]{2,1,0:T(8,128)(2,1)}), bf16[4,512,512]{2,1,0:T(8,128)(2,1)S(1)}, u32[]{:S(2)}, u32[]{:S(2)}) async-start(bf16[4,512,512]{2,1,0:T(8,128)(2,1)} %spread.1), calls=%async_computation | async-start | bytes 4194304 | tf_op jit(solution)/shard_map/all_to_all | solution.py:225
  63.5 10.8 %collective-permute-start.10 = (f32[8,128]{1,0:T(8,128)S(1)}, f32[8,128]{1,0:T(8,128)S(1)}, u32[]{:S(2)}, u32[]{:S(2)}) collective-permute-start(f32[8,128]{1,0:T(8,128)S(1)} %add.25), channel_id=1, source_target_pairs={{0,7},{1,6},{2,5},{3,4},{4,3},{5,2},{6,1},{7,0},{8,15},{9,14},{10,... | collective-permute-start | bytes 12296 | tf_op jit(solution)/shard_map/ppermute | solution.py:25
  74.3 8.5 %collective-permute-start.11 = (f32[8,128]{1,0:T(8,128)S(1)}, f32[8,128]{1,0:T(8,128)S(1)}, u32[]{:S(2)}, u32[]{:S(2)}) collective-permute-start(f32[8,128]{1,0:T(8,128)S(1)} %add.28), channel_id=1, source_target_pairs={{0,112},{8,120},{16,96},{24,104},{32,80},{40,88},{48,64},{56,72},{... | collective-permute-start | bytes 12296 | tf_op jit(solution)/shard_map/ppermute | solution.py:25
  82.8 5.5 %collective-permute-start.12 = (f32[8,128]{1,0:T(8,128)S(1)}, f32[8,128]{1,0:T(8,128)S(1)}, u32[]{:S(2)}, u32[]{:S(2)}) collective-permute-start(f32[8,128]{1,0:T(8,128)S(1)} %add.29), channel_id=1, source_target_pairs={{0,128},{8,136},{16,144},{24,152},{32,160},{40,168},{48,176},{56,1... | collective-permute-start | bytes 12296 | tf_op jit(solution)/shard_map/ppermute | solution.py:25
  88.3 8.9 %collective-permute-start.14 = (bf16[4,512,512]{2,1,0:T(8,128)(2,1)S(1)}, bf16[4,512,512]{2,1,0:T(8,128)(2,1)S(1)}, u32[]{:S(2)}, u32[]{:S(2)}) collective-permute-start(bf16[4,512,512]{2,1,0:T(8,128)(2,1)S(1)} %all-to-all-done.refs_0_), channel_id=1, source_target_pairs={{0,8},{8,0},{16,24},{24,16},{32,40},{40,32},{48,56},{56,48},{64,72... | collective-permute-start | bytes 6291464 | tf_op jit(solution)/shard_map/ppermute | solution.py:25
  90.2 7.0 %collective-permute-start.13 = (f32[8,128]{1,0:T(8,128)S(1)}, f32[8,128]{1,0:T(8,128)S(1)}, u32[]{:S(2)}, u32[]{:S(2)}) collective-permute-start(f32[8,128]{1,0:T(8,128)S(1)} %add.30), channel_id=1, source_target_pairs={{0,256},{8,264},{16,272},{24,280},{32,288},{40,296},{48,304},{56,3... | collective-permute-start | bytes 12296 | tf_op jit(solution)/shard_map/ppermute | solution.py:25

commit v4 on v3

--- a/solution.py
+++ b/solution.py
@@ -144,10 +144,16 @@
     )(position, steps, *pieces)
 
 
-def spread_kernel(half, mirrored, out):
+def spread_kernel(half, mirrored, out, sems):
+    copies = []
     for column in range(COLUMNS):
-        out[column, 0:HALF, :] = half[...]
-        out[column, HALF:, :] = mirrored[...]
+        for side, source in enumerate((half, mirrored)):
+            rows = pl.ds(side * HALF, HALF)
+            copy = pltpu.make_async_copy(source, out.at[column, rows], sems.at[2 * column + side])
+            copy.start()
+            copies.append(copy)
+    for copy in copies:
+        copy.wait()
 
 
 def spread(half, mirrored):
@@ -155,7 +161,8 @@
         spread_kernel,
         out_shape=jax.ShapeDtypeStruct((COLUMNS, ORDER, ORDER), jnp.bfloat16),
         in_specs=[VMEM] * 2,
-        out_specs=VMEM,
+        out_specs=HBM,
+        scratch_shapes=[pltpu.SemaphoreType.DMA((2 * COLUMNS,))],
         compiler_params=PARAMS,
         name="spread",
     )(half, mirrored)

time: 100 us -> 98.7 us (0.987)
  the two profiles are of different devices: /device:TPU:18 before, /device:TPU:16 now
where the time goes in v4:
time: 98.7 us; the launch traced here: 98.9 us
  starting transfers between devices  64.8 us (66%)
  waiting for transfers between devices  20.4 us (21%)
  Pallas kernels  9.76 us (10%)
  other arithmetic  1.86 us (2%)
  local copies, waits for them, and re-layouts  1.17 us (1%)
    ppermute x15, starting transfers between devices, flipped(): lax.ppermute(value, axis, [(i, i ^ mask) for i in range(lax.axis_size(axi...  60.8 us
    ppermute x15, waiting for transfers between devices, flipped(): lax.ppermute(value, axis, [(i, i ^ mask) for i in range(lax.axis_size(axi...  19 us
    pallas_call x1, Pallas kernels, refresh(): pl.pallas_call(refresh_kernel, out_shape=(jax.ShapeDtypeStruct((2, SLAB,...  6.14 us
    all_to_all x1, starting transfers between devices, per_device(): mine = lax.all_to_all(copies, 'dp', 0, 0, axis_index_groups=columns)  4.04 us
    pallas_call x1, Pallas kernels, place(): pl.pallas_call(place_kernel, out_shape=jax.ShapeDtypeStruct((1, 4 * COLUM...  2.24 us
  transfers between devices with their start and end apart: 16, of which 9 were waited for; matrix products, arithmetic and copies ran while one was open for 2% of the time, Pallas kernels for 0%

profile of v4, /device:TPU:16, one launch (start us, length us, event | category | flops | bytes accessed | tf_op | source)
XLA Modules:
  0.0 98.9 jit_solution(7229800789444220166)
XLA Ops:
  0.6 0.0 copy-start.1
  0.6 0.0 copy-start
  0.7 0.1 broadcast_in_dim.60
  0.8 0.1 broadcast_in_dim.61
  0.8 0.1 broadcast_in_dim.66
  0.9 0.1 broadcast_in_dim.67
  1.0 1.1 %fusion.1.refs_0_ = bf16[192,512]{1,0:T(8,128)(2,1)S(1)} fusion(f32[64,512]{1,0:T(8,128)} %bitcast.16, f32[64,512]{1,0:T(8,128)} %bitcast.17, pred[192]{0:T(512)(128)(4,1)S(1)} %broadcast_in_dim.67, pred[192]{0:T(512)(128)(4,1)S(1)} %broadcast_in_dim.61, bf16[64,512]{1,0:T(8,128)(2,1)} %bitcast.18), kind=kLoop, calls=%fused_computation.2 | loop fusion | flops 196608 | bytes 524672 | tf_op jit(solution)/shard_map/jit(_where)/select_n | solution.py:211
  2.1 7.6 %collective-permute-start = (bf16[192,512]{1,0:T(8,128)(2,1)S(1)}, bf16[192,512]{1,0:T(8,128)(2,1)S(1)}, u32[]{:S(2)}, u32[]{:S(2)}) collective-permute-start(bf16[192,512]{1,0:T(8,128)(2,1)S(1)} %fusion.1.refs_0_), channel_id=1, source_target_pairs={{0,32},{8,40},{16,48},{24,56},{32,0},{40,8},{48,16},{56,24},{64,96... | collective-permute-start | bytes 589832 | tf_op jit(solution)/shard_map/ppermute | solution.py:25
  9.7 1.9 %collective-permute-start.2 = (bf16[192,512]{1,0:T(8,128)(2,1)S(1)}, bf16[192,512]{1,0:T(8,128)(2,1)S(1)}, u32[]{:S(2)}, u32[]{:S(2)}) collective-permute-start(bf16[192,512]{1,0:T(8,128)(2,1)S(1)} %fusion.1.refs_0_), channel_id=1, source_target_pairs={{0,16},{8,24},{16,0},{24,8},{32,48},{40,56},{48,32},{56,40},{64,80... | collective-permute-start | bytes 589832 | tf_op jit(solution)/shard_map/ppermute | solution.py:25
  11.6 0.8 copy.8
  12.4 0.1 reshape.29.steps
  12.5 2.3 %collective-permute-done.refs_4_ = bf16[192,512]{1,0:T(8,128)(2,1)S(1)} collective-permute-done((bf16[192,512]{1,0:T(8,128)(2,1)S(1)}, bf16[192,512]{1,0:T(8,128)(2,1)S(1)}, u32[]{:S(2)}, u32[]{:S(2)}) %collective-permute-start) | collective-permute-done | bytes 196640 | tf_op jit(solution)/shard_map/ppermute | solution.py:25
  14.7 4.5 %collective-permute-start.5 = (bf16[192,512]{1,0:T(8,128)(2,1)S(1)}, bf16[192,512]{1,0:T(8,128)(2,1)S(1)}, u32[]{:S(2)}, u32[]{:S(2)}) collective-permute-start(bf16[192,512]{1,0:T(8,128)(2,1)S(1)} %collective-permute-done.refs_4_), channel_id=1, source_target_pairs={{0,16},{8,24},{16,0},{24,8},{32,48},{40,56},{48,32},{56,40},{64,80... | collective-permute-start | bytes 589832 | tf_op jit(solution)/shard_map/ppermute | solution.py:25
  19.3 1.9 %collective-permute-start.1 = (bf16[192,512]{1,0:T(8,128)(2,1)S(1)}, bf16[192,512]{1,0:T(8,128)(2,1)S(1)}, u32[]{:S(2)}, u32[]{:S(2)}) collective-permute-start(bf16[192,512]{1,0:T(8,128)(2,1)S(1)} %fusion.1.refs_0_), channel_id=1, source_target_pairs={{0,8},{8,0},{16,24},{24,16},{32,40},{40,32},{48,56},{56,48},{64,72... | collective-permute-start | bytes 589832 | tf_op jit(solution)/shard_map/ppermute | solution.py:25
  21.2 2.4 %collective-permute-start.4 = (bf16[192,512]{1,0:T(8,128)(2,1)S(1)}, bf16[192,512]{1,0:T(8,128)(2,1)S(1)}, u32[]{:S(2)}, u32[]{:S(2)}) collective-permute-start(bf16[192,512]{1,0:T(8,128)(2,1)S(1)} %collective-permute-done.refs_4_), channel_id=1, source_target_pairs={{0,8},{8,0},{16,24},{24,16},{32,40},{40,32},{48,56},{56,48},{64,72... | collective-permute-start | bytes 589832 | tf_op jit(solution)/shard_map/ppermute | solution.py:25
  23.6 0.0 collective-permute-done.2.refs_2_
  23.6 1.9 %collective-permute-start.3 = (bf16[192,512]{1,0:T(8,128)(2,1)S(1)}, bf16[192,512]{1,0:T(8,128)(2,1)S(1)}, u32[]{:S(2)}, u32[]{:S(2)}) collective-permute-start(bf16[192,512]{1,0:T(8,128)(2,1)S(1)} %collective-permute-done.2.refs_2_), channel_id=1, source_target_pairs={{0,8},{8,0},{16,24},{24,16},{32,40},{40,32},{48,56},{56,48},{64,72... | collective-permute-start | bytes 589832 | tf_op jit(solution)/shard_map/ppermute | solution.py:25
  25.5 0.0 collective-permute-done.5.refs_6_
  25.6 2.4 %collective-permute-start.6 = (bf16[192,512]{1,0:T(8,128)(2,1)S(1)}, bf16[192,512]{1,0:T(8,128)(2,1)S(1)}, u32[]{:S(2)}, u32[]{:S(2)}) collective-permute-start(bf16[192,512]{1,0:T(8,128)(2,1)S(1)} %collective-permute-done.5.refs_6_), channel_id=1, source_target_pairs={{0,8},{8,0},{16,24},{24,16},{32,40},{40,32},{48,56},{56,48},{64,72... | collective-permute-start | bytes 589832 | tf_op jit(solution)/shard_map/ppermute | solution.py:25
  28.0 0.0 collective-permute-done.1.refs_1_
  28.0 0.0 collective-permute-done.3.refs_3_
  28.0 0.0 collective-permute-done.4.refs_5_
  28.0 1.0 %collective-permute-done.6.refs_7_ = bf16[192,512]{1,0:T(8,128)(2,1)S(1)} collective-permute-done((bf16[192,512]{1,0:T(8,128)(2,1)S(1)}, bf16[192,512]{1,0:T(8,128)(2,1)S(1)}, u32[]{:S(2)}, u32[]{:S(2)}) %collective-permute-start.6) | collective-permute-done | bytes 196640 | tf_op jit(solution)/shard_map/ppermute | solution.py:25
  29.0 6.1 %refresh.1 = (f32[2,64,512]{2,1,0:T(8,128)S(1)}, bf16[256,512]{1,0:T(8,128)(2,1)S(1)}, f32[8,128]{1,0:T(8,128)S(1)}) custom-call(s32[1]{0:T(128)} %bitcast.position, s32[16]{0:T(128)S(1)} %reshape.29.steps, bf16[192,512]{1,0:T(8,128)(2,1)S(1)} %fusion.1.refs_0_, bf16[192,512]{1,0:T(8,128)(2,1)S(1)} %collective-permute-done.1.refs_1_, ...), custom_call_target="tpu_custom_call" | custom-call | tf_op jit(solution)/shard_map/refresh/pallas_call | solution.py:132
  35.2 4.3 %collective-permute-start.7 = (bf16[256,512]{1,0:T(8,128)(2,1)S(1)}, bf16[256,512]{1,0:T(8,128)(2,1)S(1)}, u32[]{:S(2)}, u32[]{:S(2)}) collective-permute-start(bf16[256,512]{1,0:T(8,128)(2,1)S(1)} %get-tuple-element.16.half), channel_id=1, source_target_pairs={{0,112},{8,120},{16,96},{24,104},{32,80},{40,88},{48,64},{56,72},{... | collective-permute-start | bytes 786440 | tf_op jit(solution)/shard_map/ppermute | solution.py:25
  39.5 4.4 %collective-permute-start.8 = (f32[8,128]{1,0:T(8,128)S(1)}, f32[8,128]{1,0:T(8,128)S(1)}, u32[]{:S(2)}, u32[]{:S(2)}) collective-permute-start(f32[8,128]{1,0:T(8,128)S(1)} %get-tuple-element.17), channel_id=1, source_target_pairs={{0,1},{1,0},{2,3},{3,2},{4,5},{5,4},{6,7},{7,6},{8,9},{9,8},{10,11... | collective-permute-start | bytes 12296 | tf_op jit(solution)/shard_map/ppermute | solution.py:25
  43.9 1.6 %collective-permute-done.8 = f32[8,128]{1,0:T(8,128)S(1)} collective-permute-done((f32[8,128]{1,0:T(8,128)S(1)}, f32[8,128]{1,0:T(8,128)S(1)}, u32[]{:S(2)}, u32[]{:S(2)}) %collective-permute-start.8) | collective-permute-done | bytes 4128 | tf_op jit(solution)/shard_map/ppermute | solution.py:25
  45.5 10.1 %collective-permute-start.9 = (f32[8,128]{1,0:T(8,128)S(1)}, f32[8,128]{1,0:T(8,128)S(1)}, u32[]{:S(2)}, u32[]{:S(2)}) collective-permute-start(f32[8,128]{1,0:T(8,128)S(1)} %add.24), channel_id=1, source_target_pairs={{0,2},{1,3},{2,0},{3,1},{4,6},{5,7},{6,4},{7,5},{8,10},{9,11},{10,... | collective-permute-start | bytes 12296 | tf_op jit(solution)/shard_map/ppermute | solution.py:25
  55.6 0.0 copy-done.1
  55.6 0.0 copy-done
  55.6 0.7 slice_add_fusion
  56.3 0.8 collective-permute-done.9
  57.2 0.0 collective-permute-done.7.mirrored
  57.2 1.4 %spread.1 = bf16[4,512,512]{2,1,0:T(8,128)(2,1)} custom-call(bf16[256,512]{1,0:T(8,128)(2,1)S(1)} %get-tuple-element.16.half, bf16[256,512]{1,0:T(8,128)(2,1)S(1)} %collective-permute-done.7.mirrored), custom_call_target="tpu_custom_call" | custom-call | tf_op jit(solution)/shard_map/spread/pallas_call | solution.py:160
  58.6 4.0 %all-to-all-start = ((bf16[4,512,512]{2,1,0:T(8,128)(2,1)}), bf16[4,512,512]{2,1,0:T(8,128)(2,1)S(1)}, u32[]{:S(2)}, u32[]{:S(2)}) async-start(bf16[4,512,512]{2,1,0:T(8,128)(2,1)} %spread.1), calls=%async_computation | async-start | bytes 4194304 | tf_op jit(solution)/shard_map/all_to_all | solution.py:232
  62.6 6.9 %collective-permute-start.10 = (f32[8,128]{1,0:T(8,128)S(1)}, f32[8,128]{1,0:T(8,128)S(1)}, u32[]{:S(2)}, u32[]{:S(2)}) collective-permute-start(f32[8,128]{1,0:T(8,128)S(1)} %add.25), channel_id=1, source_target_pairs={{0,7},{1,6},{2,5},{3,4},{4,3},{5,2},{6,1},{7,0},{8,15},{9,14},{10,... | collective-permute-start | bytes 12296 | tf_op jit(solution)/shard_map/ppermute | solution.py:25
  69.5 1.6 %collective-permute-done.10 = f32[8,128]{1,0:T(8,128)S(1)} collective-permute-done((f32[8,128]{1,0:T(8,128)S(1)}, f32[8,128]{1,0:T(8,128)S(1)}, u32[]{:S(2)}, u32[]{:S(2)}) %collective-permute-start.10) | collective-permute-done | bytes 4128 | tf_op jit(solution)/shard_map/ppermute | solution.py:25
  71.1 3.4 %collective-permute-start.11 = (f32[8,128]{1,0:T(8,128)S(1)}, f32[8,128]{1,0:T(8,128)S(1)}, u32[]{:S(2)}, u32[]{:S(2)}) collective-permute-start(f32[8,128]{1,0:T(8,128)S(1)} %add.28), channel_id=1, source_target_pairs={{0,112},{8,120},{16,96},{24,104},{32,80},{40,88},{48,64},{56,72},{... | collective-permute-start | bytes 12296 | tf_op jit(solution)/shard_map/ppermute | solution.py:25
  74.5 5.1 %collective-permute-done.11 = f32[8,128]{1,0:T(8,128)S(1)} collective-permute-done((f32[8,128]{1,0:T(8,128)S(1)}, f32[8,128]{1,0:T(8,128)S(1)}, u32[]{:S(2)}, u32[]{:S(2)}) %collective-permute-start.11) | collective-permute-done | bytes 4128 | tf_op jit(solution)/shard_map/ppermute | solution.py:25
  79.6 3.9 %collective-permute-start.12 = (f32[8,128]{1,0:T(8,128)S(1)}, f32[8,128]{1,0:T(8,128)S(1)}, u32[]{:S(2)}, u32[]{:S(2)}) collective-permute-start(f32[8,128]{1,0:T(8,128)S(1)} %add.29), channel_id=1, source_target_pairs={{0,128},{8,136},{16,144},{24,152},{32,160},{40,168},{48,176},{56,1... | collective-permute-start | bytes 12296 | tf_op jit(solution)/shard_map/ppermute | solution.py:25
  83.5 2.7 %collective-permute-done.12 = f32[8,128]{1,0:T(8,128)S(1)} collective-permute-done((f32[8,128]{1,0:T(8,128)S(1)}, f32[8,128]{1,0:T(8,128)S(1)}, u32[]{:S(2)}, u32[]{:S(2)}) %collective-permute-start.12) | collective-permute-done | bytes 4128 | tf_op jit(solution)/shard_map/ppermute | solution.py:25
  86.3 1.5 %all-to-all-done.refs_0_ = bf16[4,512,512]{2,1,0:T(8,128)(2,1)S(1)} async-done(((bf16[4,512,512]{2,1,0:T(8,128)(2,1)}), bf16[4,512,512]{2,1,0:T(8,128)(2,1)S(1)}, u32[]{:S(2)}, u32[]{:S(2)}) %all-to-all-start) | async-done | bytes 2097184 | tf_op jit(solution)/shard_map/all_to_all | solution.py:232
  87.8 1.9 %collective-permute-start.14 = (bf16[4,512,512]{2,1,0:T(8,128)(2,1)S(1)}, bf16[4,512,512]{2,1,0:T(8,128)(2,1)S(1)}, u32[]{:S(2)}, u32[]{:S(2)}) collective-permute-start(bf16[4,512,512]{2,1,0:T(8,128)(2,1)S(1)} %all-to-all-done.refs_0_), channel_id=1, source_target_pairs={{0,8},{8,0},{16,24},{24,16},{32,40},{40,32},{48,56},{56,48},{64,72... | collective-permute-start | bytes 6291464 | tf_op jit(solution)/shard_map/ppermute | solution.py:25
  89.7 3.1 %collective-permute-start.13 = (f32[8,128]{1,0:T(8,128)S(1)}, f32[8,128]{1,0:T(8,128)S(1)}, u32[]{:S(2)}, u32[]{:S(2)}) collective-permute-start(f32[8,128]{1,0:T(8,128)S(1)} %add.30), channel_id=1, source_target_pairs={{0,256},{8,264},{16,272},{24,280},{32,288},{40,296},{48,304},{56,3... | collective-permute-start | bytes 12296 | tf_op jit(solution)/shard_map/ppermute | solution.py:25
  92.8 3.9 %collective-permute-done.13 = f32[8,128]{1,0:T(8,128)S(1)} collective-permute-done((f32[8,128]{1,0:T(8,128)S(1)}, f32[8,128]{1,0:T(8,128)S(1)}, u32[]{:S(2)}, u32[]{:S(2)}) %collective-permute-start.13) | collective-permute-done | bytes 4128 | tf_op jit(solution)/shard_map/ppermute | solution.py:25
  96.7 0.0 collective-permute-done.14.refs_1_
  96.7 2.2 %place.1 = bf16[1,4096,512]{2,1,0:T(8,128)(2,1)} custom-call(s32[1]{0:T(128)} %bitcast.position, f32[8,128]{1,0:T(8,128)S(1)} %add.31.sums, bf16[4,512,512]{2,1,0:T(8,128)(2,1)S(1)} %all-to-all-done.refs_0_, bf16[4,512,512]{2,1,0:T(8,128)(2,1)S(1)} %collective-permute-done.14.refs_1_), custom_call_target="tpu_custom_call" | custom-call | tf_op jit(solution)/shard_map/place/pallas_call | solution.py:192
  (8 shorter events, 0.0 us)
Async XLA Ops:
  0.6 55.0 %copy-start.1 = (f32[1,64,512]{2,1,0:T(8,128)S(1)}, f32[1,64,512]{2,1,0:T(8,128)}, u32[]{:S(2)}) copy-start(f32[1,64,512]{2,1,0:T(8,128)} %param.5) | copy-start | bytes 393220
  0.6 55.0 %copy-start = (f32[1,64,512]{2,1,0:T(8,128)S(1)}, f32[1,64,512]{2,1,0:T(8,128)}, u32[]{:S(2)}) copy-start(f32[1,64,512]{2,1,0:T(8,128)} %param.6) | copy-start | bytes 393220
  2.1 12.7 %collective-permute-start = (bf16[192,512]{1,0:T(8,128)(2,1)S(1)}, bf16[192,512]{1,0:T(8,128)(2,1)S(1)}, u32[]{:S(2)}, u32[]{:S(2)}) collective-permute-start(bf16[192,512]{1,0:T(8,128)(2,1)S(1)} %fusion.1.refs_0_), channel_id=1, source_target_pairs={{0,32},{8,40},{16,48},{24,56},{32,0},{40,8},{48,16},{56,24},{64,96... | collective-permute-start | bytes 589832 | tf_op jit(solution)/shard_map/ppermute | solution.py:25
  9.7 13.9 %collective-permute-start.2 = (bf16[192,512]{1,0:T(8,128)(2,1)S(1)}, bf16[192,512]{1,0:T(8,128)(2,1)S(1)}, u32[]{:S(2)}, u32[]{:S(2)}) collective-permute-start(bf16[192,512]{1,0:T(8,128)(2,1)S(1)} %fusion.1.refs_0_), channel_id=1, source_target_pairs={{0,16},{8,24},{16,0},{24,8},{32,48},{40,56},{48,32},{56,40},{64,80... | collective-permute-start | bytes 589832 | tf_op jit(solution)/shard_map/ppermute | solution.py:25
  14.7 10.8 %collective-permute-start.5 = (bf16[192,512]{1,0:T(8,128)(2,1)S(1)}, bf16[192,512]{1,0:T(8,128)(2,1)S(1)}, u32[]{:S(2)}, u32[]{:S(2)}) collective-permute-start(bf16[192,512]{1,0:T(8,128)(2,1)S(1)} %collective-permute-done.refs_4_), channel_id=1, source_target_pairs={{0,16},{8,24},{16,0},{24,8},{32,48},{40,56},{48,32},{56,40},{64,80... | collective-permute-start | bytes 589832 | tf_op jit(solution)/shard_map/ppermute | solution.py:25
  19.3 8.7 %collective-permute-start.1 = (bf16[192,512]{1,0:T(8,128)(2,1)S(1)}, bf16[192,512]{1,0:T(8,128)(2,1)S(1)}, u32[]{:S(2)}, u32[]{:S(2)}) collective-permute-start(bf16[192,512]{1,0:T(8,128)(2,1)S(1)} %fusion.1.refs_0_), channel_id=1, source_target_pairs={{0,8},{8,0},{16,24},{24,16},{32,40},{40,32},{48,56},{56,48},{64,72... | collective-permute-start | bytes 589832 | tf_op jit(solution)/shard_map/ppermute | solution.py:25
  21.2 6.8 %collective-permute-start.4 = (bf16[192,512]{1,0:T(8,128)(2,1)S(1)}, bf16[192,512]{1,0:T(8,128)(2,1)S(1)}, u32[]{:S(2)}, u32[]{:S(2)}) collective-permute-start(bf16[192,512]{1,0:T(8,128)(2,1)S(1)} %collective-permute-done.refs_4_), channel_id=1, source_target_pairs={{0,8},{8,0},{16,24},{24,16},{32,40},{40,32},{48,56},{56,48},{64,72... | collective-permute-start | bytes 589832 | tf_op jit(solution)/shard_map/ppermute | solution.py:25
  23.6 4.4 %collective-permute-start.3 = (bf16[192,512]{1,0:T(8,128)(2,1)S(1)}, bf16[192,512]{1,0:T(8,128)(2,1)S(1)}, u32[]{:S(2)}, u32[]{:S(2)}) collective-permute-start(bf16[192,512]{1,0:T(8,128)(2,1)S(1)} %collective-permute-done.2.refs_2_), channel_id=1, source_target_pairs={{0,8},{8,0},{16,24},{24,16},{32,40},{40,32},{48,56},{56,48},{64,72... | collective-permute-start | bytes 589832 | tf_op jit(solution)/shard_map/ppermute | solution.py:25
  25.6 3.5 %collective-permute-start.6 = (bf16[192,512]{1,0:T(8,128)(2,1)S(1)}, bf16[192,512]{1,0:T(8,128)(2,1)S(1)}, u32[]{:S(2)}, u32[]{:S(2)}) collective-permute-start(bf16[192,512]{1,0:T(8,128)(2,1)S(1)} %collective-permute-done.5.refs_6_), channel_id=1, source_target_pairs={{0,8},{8,0},{16,24},{24,16},{32,40},{40,32},{48,56},{56,48},{64,72... | collective-permute-start | bytes 589832 | tf_op jit(solution)/shard_map/ppermute | solution.py:25
  35.2 22.0 %collective-permute-start.7 = (bf16[256,512]{1,0:T(8,128)(2,1)S(1)}, bf16[256,512]{1,0:T(8,128)(2,1)S(1)}, u32[]{:S(2)}, u32[]{:S(2)}) collective-permute-start(bf16[256,512]{1,0:T(8,128)(2,1)S(1)} %get-tuple-element.16.half), channel_id=1, source_target_pairs={{0,112},{8,120},{16,96},{24,104},{32,80},{40,88},{48,64},{56,72},{... | collective-permute-start | bytes 786440 | tf_op jit(solution)/shard_map/ppermute | solution.py:25
  39.5 6.0 %collective-permute-start.8 = (f32[8,128]{1,0:T(8,128)S(1)}, f32[8,128]{1,0:T(8,128)S(1)}, u32[]{:S(2)}, u32[]{:S(2)}) collective-permute-start(f32[8,128]{1,0:T(8,128)S(1)} %get-tuple-element.17), channel_id=1, source_target_pairs={{0,1},{1,0},{2,3},{3,2},{4,5},{5,4},{6,7},{7,6},{8,9},{9,8},{10,11... | collective-permute-start | bytes 12296 | tf_op jit(solution)/shard_map/ppermute | solution.py:25
  45.5 11.7 %collective-permute-start.9 = (f32[8,128]{1,0:T(8,128)S(1)}, f32[8,128]{1,0:T(8,128)S(1)}, u32[]{:S(2)}, u32[]{:S(2)}) collective-permute-start(f32[8,128]{1,0:T(8,128)S(1)} %add.24), channel_id=1, source_target_pairs={{0,2},{1,3},{2,0},{3,1},{4,6},{5,7},{6,4},{7,5},{8,10},{9,11},{10,... | collective-permute-start | bytes 12296 | tf_op jit(solution)/shard_map/ppermute | solution.py:25
  58.6 29.2 %all-to-all-start = ((bf16[4,512,512]{2,1,0:T(8,128)(2,1)}), bf16[4,512,512]{2,1,0:T(8,128)(2,1)S(1)}, u32[]{:S(2)}, u32[]{:S(2)}) async-start(bf16[4,512,512]{2,1,0:T(8,128)(2,1)} %spread.1), calls=%async_computation | async-start | bytes 4194304 | tf_op jit(solution)/shard_map/all_to_all | solution.py:232
  62.6 8.5 %collective-permute-start.10 = (f32[8,128]{1,0:T(8,128)S(1)}, f32[8,128]{1,0:T(8,128)S(1)}, u32[]{:S(2)}, u32[]{:S(2)}) collective-permute-start(f32[8,128]{1,0:T(8,128)S(1)} %add.25), channel_id=1, source_target_pairs={{0,7},{1,6},{2,5},{3,4},{4,3},{5,2},{6,1},{7,0},{8,15},{9,14},{10,... | collective-permute-start | bytes 12296 | tf_op jit(solution)/shard_map/ppermute | solution.py:25
  71.1 8.5 %collective-permute-start.11 = (f32[8,128]{1,0:T(8,128)S(1)}, f32[8,128]{1,0:T(8,128)S(1)}, u32[]{:S(2)}, u32[]{:S(2)}) collective-permute-start(f32[8,128]{1,0:T(8,128)S(1)} %add.28), channel_id=1, source_target_pairs={{0,112},{8,120},{16,96},{24,104},{32,80},{40,88},{48,64},{56,72},{... | collective-permute-start | bytes 12296 | tf_op jit(solution)/shard_map/ppermute | solution.py:25
  79.6 6.7 %collective-permute-start.12 = (f32[8,128]{1,0:T(8,128)S(1)}, f32[8,128]{1,0:T(8,128)S(1)}, u32[]{:S(2)}, u32[]{:S(2)}) collective-permute-start(f32[8,128]{1,0:T(8,128)S(1)} %add.29), channel_id=1, source_target_pairs={{0,128},{8,136},{16,144},{24,152},{32,160},{40,168},{48,176},{56,1... | collective-permute-start | bytes 12296 | tf_op jit(solution)/shard_map/ppermute | solution.py:25
  87.8 8.9 %collective-permute-start.14 = (bf16[4,512,512]{2,1,0:T(8,128)(2,1)S(1)}, bf16[4,512,512]{2,1,0:T(8,128)(2,1)S(1)}, u32[]{:S(2)}, u32[]{:S(2)}) collective-permute-start(bf16[4,512,512]{2,1,0:T(8,128)(2,1)S(1)} %all-to-all-done.refs_0_), channel_id=1, source_target_pairs={{0,8},{8,0},{16,24},{24,16},{32,40},{40,32},{48,56},{56,48},{64,72... | collective-permute-start | bytes 6291464 | tf_op jit(solution)/shard_map/ppermute | solution.py:25
  89.7 7.0 %collective-permute-start.13 = (f32[8,128]{1,0:T(8,128)S(1)}, f32[8,128]{1,0:T(8,128)S(1)}, u32[]{:S(2)}, u32[]{:S(2)}) collective-permute-start(f32[8,128]{1,0:T(8,128)S(1)} %add.30), channel_id=1, source_target_pairs={{0,256},{8,264},{16,272},{24,280},{32,288},{40,296},{48,304},{56,3... | collective-permute-start | bytes 12296 | tf_op jit(solution)/shard_map/ppermute | solution.py:25
